TPU v7x, 256 devices: a whole 4x4x8 slice. The times are simulated.
256 devices in a mesh: aux: 16 (over y, x_lo, core), bas: 16 (over z, x_hi).
Axes of the slice: x: 4 (x_hi: 2, x_lo: 2; x = x_hi * 2 + x_lo), y: 4, z: 8, core: 2. Of those that a mesh axis runs over, the one named last changes fastest.
Arguments:
- factors: float32 [16, 8192, 1024], P('aux', 'bas'), may hold values from -0.8 to 0.8
Outputs:
- k_tiles: float32 [16, 512, 9, 512], P('bas', 'aux')
All inputs are finite; a program needn't handle non-finite values.
Results may differ from a plain program's by a relative error of at most 0.0003.
Values sent between devices are 32-bit elements; how exact they have to be, the bound alone decides.
No kernel may reach another device: no remote copies, remote signals or barrier semaphores. Data moves between devices by JAX's collectives and lax.ppermute only.
A program may use at most 128 MiB of HBM per device.

v0:
```python
import jax
import jax.numpy as jnp
from jax import lax
from jax.sharding import PartitionSpec as P


def passed_along(shard, axis, by):
    peers = lax.axis_size(axis)
    return lax.ppermute(shard, axis, [(i, (i + by) % peers) for i in range(peers)])


def products(own_rows, stacked):
    return lax.dot_general(
        own_rows,
        stacked,
        (((0, 2), (1, 3)), ((), ())),
        precision=lax.Precision.HIGHEST,
        preferred_element_type=jnp.float32,
    )


def body(factors):
    count_bas = lax.axis_size("bas")
    count_aux = lax.axis_size("aux")
    offsets = count_bas // 2 + 1
    blocks = [factors]
    current = factors
    for offset in range(1, offsets):
        current = passed_along(current, "bas", -1)
        blocks.append(current)
    stacked = jnp.stack(blocks, axis=0)
    tile_rows = factors.shape[1]
    share = tile_rows // count_aux
    partial_value = products(factors, stacked)
    summed = lax.psum_scatter(partial_value, "aux", scatter_dimension=0, tiled=True)
    return summed.reshape(1, share, offsets, tile_rows)


def solution(mesh):
    return jax.shard_map(
        body,
        mesh=mesh,
        in_specs=(P("aux", "bas", None),),
        out_specs=P("bas", "aux", None, None),
        check_vma=False,
    )
```

profile of v0, /device:TPU:4, one launch (start us, length us, event | category | flops | bytes accessed | tf_op | source)
XLA Modules:
  0.0 634.6 jit_solution(12564909514960789958)
XLA Ops:
  6.5 0.0 copy-start
  6.5 0.0 reduce-scatter.2.cloned.1.call-start
  6.5 2.2 collective-permute-start
  8.8 47.7 %collective-permute-done = f32[1,512,1024]{2,1,0:T(8,128)S(1)} collective-permute-done((f32[1,512,1024]{2,1,0:T(8,128)}, f32[1,512,1024]{2,1,0:T(8,128)S(1)}, u32[]{:S(2)}, u32[]{:S(2)}) %collective-permute-start) | collective-permute-done | bytes 2097184 | tf_op jit(solution)/shard_map/ppermute | solution.py:9
  56.5 4.0 collective-permute-start.1
  60.6 44.9 %collective-permute-done.1 = f32[1,512,1024]{2,1,0:T(8,128)S(1)} collective-permute-done((f32[1,512,1024]{2,1,0:T(8,128)S(1)}, f32[1,512,1024]{2,1,0:T(8,128)S(1)}, u32[]{:S(2)}, u32[]{:S(2)}) %collective-permute-start.1) | collective-permute-done | bytes 2097184 | tf_op jit(solution)/shard_map/ppermute | solution.py:9
  105.4 5.1 collective-permute-start.2
  110.6 43.1 %collective-permute-done.2 = f32[1,512,1024]{2,1,0:T(8,128)S(1)} collective-permute-done((f32[1,512,1024]{2,1,0:T(8,128)S(1)}, f32[1,512,1024]{2,1,0:T(8,128)S(1)}, u32[]{:S(2)}, u32[]{:S(2)}) %collective-permute-start.2) | collective-permute-done | bytes 2097184 | tf_op jit(solution)/shard_map/ppermute | solution.py:9
  153.7 6.1 collective-permute-start.3
  159.8 42.2 %collective-permute-done.3 = f32[1,512,1024]{2,1,0:T(8,128)S(1)} collective-permute-done((f32[1,512,1024]{2,1,0:T(8,128)S(1)}, f32[1,512,1024]{2,1,0:T(8,128)S(1)}, u32[]{:S(2)}, u32[]{:S(2)}) %collective-permute-start.3) | collective-permute-done | bytes 2097184 | tf_op jit(solution)/shard_map/ppermute | solution.py:9
  201.9 6.1 collective-permute-start.4
  208.0 41.3 %collective-permute-done.4 = f32[1,512,1024]{2,1,0:T(8,128)S(1)} collective-permute-done((f32[1,512,1024]{2,1,0:T(8,128)S(1)}, f32[1,512,1024]{2,1,0:T(8,128)S(1)}, u32[]{:S(2)}, u32[]{:S(2)}) %collective-permute-start.4) | collective-permute-done | bytes 2097184 | tf_op jit(solution)/shard_map/ppermute | solution.py:9
  249.3 6.1 collective-permute-start.5
  255.4 40.3 %collective-permute-done.5 = f32[1,512,1024]{2,1,0:T(8,128)S(1)} collective-permute-done((f32[1,512,1024]{2,1,0:T(8,128)S(1)}, f32[1,512,1024]{2,1,0:T(8,128)S(1)}, u32[]{:S(2)}, u32[]{:S(2)}) %collective-permute-start.5) | collective-permute-done | bytes 2097184 | tf_op jit(solution)/shard_map/ppermute | solution.py:9
  295.7 6.1 collective-permute-start.6
  301.8 1.7 bitcast_dynamic-update-slice_fusion.8
  303.5 38.0 %collective-permute-done.6 = f32[1,512,1024]{2,1,0:T(8,128)S(1)} collective-permute-done((f32[1,512,1024]{2,1,0:T(8,128)S(1)}, f32[1,512,1024]{2,1,0:T(8,128)S(1)}, u32[]{:S(2)}, u32[]{:S(2)}) %collective-permute-start.6) | collective-permute-done | bytes 2097184 | tf_op jit(solution)/shard_map/ppermute | solution.py:9
  341.5 6.1 collective-permute-start.7
  347.6 0.2 bitcast_dynamic-update-slice_fusion.6
  347.8 0.2 bitcast_dynamic-update-slice_fusion.5
  348.1 0.2 bitcast_dynamic-update-slice_fusion.4
  348.4 0.2 bitcast_dynamic-update-slice_fusion.3
  348.6 0.2 bitcast_dynamic-update-slice_fusion.2
  348.9 0.2 bitcast_dynamic-update-slice_fusion.1
  349.1 0.2 bitcast_dynamic-update-slice_fusion
  349.4 36.8 %collective-permute-done.7 = f32[1,512,1024]{2,1,0:T(8,128)S(1)} collective-permute-done((f32[1,512,1024]{2,1,0:T(8,128)S(1)}, f32[1,512,1024]{2,1,0:T(8,128)S(1)}, u32[]{:S(2)}, u32[]{:S(2)}) %collective-permute-start.7) | collective-permute-done | bytes 2097184 | tf_op jit(solution)/shard_map/ppermute | solution.py:9
  386.2 0.2 bitcast_dynamic-update-slice_fusion.7
  386.4 0.0 copy-done
  386.4 32.6 %fusion.2 = f32[512,9,512]{0,2,1:T(8,128)} fusion(f32[9,1,512,1024]{3,2,0,1:T(8,128)S(1)} %bitcast_dynamic-update-slice_fusion.7, f32[1,512,1024]{2,1,0:T(8,128)S(1)} %copy-done), kind=kOutput, calls=%fused_computation.2 | convolution fusion | flops 28991029248 | bytes 30408704 | tf_op jit(solution)/shard_map/dot_general | solution.py:13
  419.0 16.7 %copy.17 = f32[512,9,512]{2,1,0:T(8,128)} copy(f32[512,9,512]{0,2,1:T(8,128)} %fusion.2) | data formatting | bytes 18874368 | tf_op jit(solution)/shard_map/dot_general | solution.py:13
  435.7 0.0 reduce-scatter.2.cloned.1.call-update
  435.7 189.7 %reduce-scatter.2.cloned.1.call-done = f32[32,9,512]{2,1,0:T(8,128)} async-done(((f32[512,9,512]{2,1,0:T(8,128)}), f32[32,9,512]{2,1,0:T(8,128)}) %reduce-scatter.2.cloned.1.call-update) | async-done | bytes 589840 | tf_op jit(solution)/shard_map/reduce_scatter | solution.py:35
  625.4 2.4 copy.18
Async XLA Ops:
  6.5 379.9 %copy-start = (f32[1,512,1024]{2,1,0:T(8,128)S(1)}, f32[1,512,1024]{2,1,0:T(8,128)}, u32[]{:S(2)}) copy-start(f32[1,512,1024]{2,1,0:T(8,128)} %param.1) | copy-start | bytes 6291460
  6.5 618.8 %reduce-scatter.2.cloned.1.call-start = ((), (), s32[]{:S(2)}) async-start(), calls=%async_computation.1 | async-start | bytes 17825792 | tf_op jit(solution)/shard_map/reduce_scatter | solution.py:35
  6.5 50.0 %collective-permute-start = (f32[1,512,1024]{2,1,0:T(8,128)}, f32[1,512,1024]{2,1,0:T(8,128)S(1)}, u32[]{:S(2)}, u32[]{:S(2)}) collective-permute-start(f32[1,512,1024]{2,1,0:T(8,128)} %param.1), channel_id=1, source_target_pairs={{0,15},{1,0},{2,1},{3,2},{4,3},{5,4},{6,5},{7,6},{8,7},{9,8},{10,9... | collective-permute-start | bytes 6291464 | tf_op jit(solution)/shard_map/ppermute | solution.py:9
  56.5 48.9 %collective-permute-start.1 = (f32[1,512,1024]{2,1,0:T(8,128)S(1)}, f32[1,512,1024]{2,1,0:T(8,128)S(1)}, u32[]{:S(2)}, u32[]{:S(2)}) collective-permute-start(f32[1,512,1024]{2,1,0:T(8,128)S(1)} %collective-permute-done), channel_id=1, source_target_pairs={{0,15},{1,0},{2,1},{3,2},{4,3},{5,4},{6,5},{7,6},{8,7},{9,8},{10,9... | collective-permute-start | bytes 6291464 | tf_op jit(solution)/shard_map/ppermute | solution.py:9
  105.4 48.2 %collective-permute-start.2 = (f32[1,512,1024]{2,1,0:T(8,128)S(1)}, f32[1,512,1024]{2,1,0:T(8,128)S(1)}, u32[]{:S(2)}, u32[]{:S(2)}) collective-permute-start(f32[1,512,1024]{2,1,0:T(8,128)S(1)} %collective-permute-done.1), channel_id=1, source_target_pairs={{0,15},{1,0},{2,1},{3,2},{4,3},{5,4},{6,5},{7,6},{8,7},{9,8},{10,9... | collective-permute-start | bytes 6291464 | tf_op jit(solution)/shard_map/ppermute | solution.py:9
  153.7 48.3 %collective-permute-start.3 = (f32[1,512,1024]{2,1,0:T(8,128)S(1)}, f32[1,512,1024]{2,1,0:T(8,128)S(1)}, u32[]{:S(2)}, u32[]{:S(2)}) collective-permute-start(f32[1,512,1024]{2,1,0:T(8,128)S(1)} %collective-permute-done.2), channel_id=1, source_target_pairs={{0,15},{1,0},{2,1},{3,2},{4,3},{5,4},{6,5},{7,6},{8,7},{9,8},{10,9... | collective-permute-start | bytes 6291464 | tf_op jit(solution)/shard_map/ppermute | solution.py:9
  201.9 47.3 %collective-permute-start.4 = (f32[1,512,1024]{2,1,0:T(8,128)S(1)}, f32[1,512,1024]{2,1,0:T(8,128)S(1)}, u32[]{:S(2)}, u32[]{:S(2)}) collective-permute-start(f32[1,512,1024]{2,1,0:T(8,128)S(1)} %collective-permute-done.3), channel_id=1, source_target_pairs={{0,15},{1,0},{2,1},{3,2},{4,3},{5,4},{6,5},{7,6},{8,7},{9,8},{10,9... | collective-permute-start | bytes 6291464 | tf_op jit(solution)/shard_map/ppermute | solution.py:9
  249.3 46.4 %collective-permute-start.5 = (f32[1,512,1024]{2,1,0:T(8,128)S(1)}, f32[1,512,1024]{2,1,0:T(8,128)S(1)}, u32[]{:S(2)}, u32[]{:S(2)}) collective-permute-start(f32[1,512,1024]{2,1,0:T(8,128)S(1)} %collective-permute-done.4), channel_id=1, source_target_pairs={{0,15},{1,0},{2,1},{3,2},{4,3},{5,4},{6,5},{7,6},{8,7},{9,8},{10,9... | collective-permute-start | bytes 6291464 | tf_op jit(solution)/shard_map/ppermute | solution.py:9
  295.7 45.8 %collective-permute-start.6 = (f32[1,512,1024]{2,1,0:T(8,128)S(1)}, f32[1,512,1024]{2,1,0:T(8,128)S(1)}, u32[]{:S(2)}, u32[]{:S(2)}) collective-permute-start(f32[1,512,1024]{2,1,0:T(8,128)S(1)} %collective-permute-done.5), channel_id=1, source_target_pairs={{0,15},{1,0},{2,1},{3,2},{4,3},{5,4},{6,5},{7,6},{8,7},{9,8},{10,9... | collective-permute-start | bytes 6291464 | tf_op jit(solution)/shard_map/ppermute | solution.py:9
  341.5 44.6 %collective-permute-start.7 = (f32[1,512,1024]{2,1,0:T(8,128)S(1)}, f32[1,512,1024]{2,1,0:T(8,128)S(1)}, u32[]{:S(2)}, u32[]{:S(2)}) collective-permute-start(f32[1,512,1024]{2,1,0:T(8,128)S(1)} %collective-permute-done.6), channel_id=1, source_target_pairs={{0,15},{1,0},{2,1},{3,2},{4,3},{5,4},{6,5},{7,6},{8,7},{9,8},{10,9... | collective-permute-start | bytes 6291464 | tf_op jit(solution)/shard_map/ppermute | solution.py:9
Sparse Core Ops, SparseCore 0:
  435.8 189.5 reduce-scatter.1
where the time goes:
time: 635 us
  waiting for transfers between devices  524 us (83%)
  starting transfers between devices  41.9 us (7%)
  matrix products  32.6 us (5%)
  local copies, waits for them, and re-layouts  22.7 us (4%)
  between operations  13.5 us (2%)
    ppermute x8, waiting for transfers between devices, passed_along(): lax.ppermute(shard, axis, [(i, (i + by) % peers) for i in range(peers)])  334 us
    reduce_scatter x1, waiting for transfers between devices, body(): lax.psum_scatter(partial_value, 'aux', scatter_dimension=0, tiled=True)  190 us
    ppermute x8, starting transfers between devices, passed_along(): lax.ppermute(shard, axis, [(i, (i + by) % peers) for i in range(peers)])  41.9 us
    dot_general x1, matrix products, products(): lax.dot_general(own_rows, stacked, (((0, 2), (1, 3)), ((), ())), precisio...  32.6 us
    dot_general x1, local copies, waits for them, and re-layouts, products(): lax.dot_general(own_rows, stacked, (((0, 2), (1, 3)), ((), ())), precisio...  16.7 us
  transfers between devices with their start and end apart: 9, of which 9 were waited for; matrix products, arithmetic and copies ran while one was open for 1% of the time, Pallas kernels for 0%

commit v1 on v0

v1 whole, which is shorter than its diff:
```python
import functools

import jax
import jax.numpy as jnp
from jax import lax
from jax.experimental import pallas as pl
from jax.experimental.pallas import tpu as pltpu
from jax.sharding import PartitionSpec as P

NY, NXL, NC, NZ, NXH = 4, 2, 2, 8, 2
TILE = 512
SHARE = 32


def place(y, xl, c, z, xh):
    return (((y % NY) * NXL + xl % NXL) * NC + c % NC) * (NZ * NXH) + (z % NZ) * NXH + xh % NXH


def send(value, target):
    pairs = []
    for y in range(NY):
        for xl in range(NXL):
            for c in range(NC):
                for z in range(NZ):
                    for xh in range(NXH):
                        to = target(y, xl, c, z, xh)
                        if to is not None:
                            pairs.append((place(y, xl, c, z, xh), place(*to)))
    return lax.ppermute(value, ("aux", "bas"), pairs)


def z_by(step):
    return lambda y, xl, c, z, xh: (y, xl, c, z + step, xh)


def y_by(step):
    return lambda y, xl, c, z, xh: (y + step, xl, c, z, xh)


def swap_core(y, xl, c, z, xh):
    return y, xl, 1 - c, z, xh


def swap_xh(y, xl, c, z, xh):
    return y, xl, c, z, 1 - xh


def call(kernel, outs, args, vmem, scratch=()):
    return pl.pallas_call(
        kernel,
        out_shape=[jax.ShapeDtypeStruct(shape, jnp.float32) for shape in outs],
        in_specs=[pl.BlockSpec(memory_space=pltpu.SMEM)] + [pl.BlockSpec(memory_space=pltpu.VMEM)] * (len(args) - 1),
        out_specs=[pl.BlockSpec(memory_space=pltpu.VMEM)] * len(outs),
        scratch_shapes=list(scratch),
        compiler_params=pltpu.CompilerParams(vmem_limit_bytes=vmem * 2**20),
        cost_estimate=pl.CostEstimate(flops=0, bytes_accessed=0, transcendentals=0),
    )(*args)


def two_terms(value):
    high = value.astype(jnp.bfloat16)
    return high, (value - high.astype(jnp.float32)).astype(jnp.bfloat16)


def products_kernel(tiles, rows, columns, count, before, place_ref, *refs):
    operands, (mine, other, row_high, row_low, column_high, column_low) = refs[:count], refs[-6:]
    y, xl, c, xh = (place_ref[i] for i in range(4))

    def split(block, high, low, i, target):
        done = 0
        for at in block:
            chunk = operands[at]
            groups = chunk.shape[0] // SHARE

            @pl.loop(0, groups)
            def _(g, chunk=chunk, done=done):
                to = pl.ds(pl.multiple_of(target(g + done) * SHARE, SHARE), SHARE)
                value = chunk[pl.ds(pl.multiple_of(g * SHARE, SHARE), SHARE), :]
                high[i, to, :], low[i, to, :] = two_terms(value)

            done += groups

    def split_either(pair, high, low, i, target):
        if pair[0] == pair[1]:
            split(pair[0], high, low, i, target)
        else:
            for column_of_chips in range(2):
                @pl.when(xh == column_of_chips)
                def _():
                    split(pair[column_of_chips], high, low, i, target)

    def row_target(g):
        return (g % 2 + 2 - c) % 2 * 8 + (g // 4 + 4 - y) % 4 * 2 + (g // 2 % 2 + 2 - xl) % 2

    if before:
        mine[:, :before] = refs[count][...]
        other[:, :before] = refs[count + 1][...]
    for i, pair in enumerate(rows):
        split_either(pair, row_high, row_low, i, row_target)
    for i, pair in enumerate(columns):
        split_either(pair, column_high, column_low, i, lambda g: g)

    def dot(a, b):
        return lax.dot_general(a, b, (((1,), (1,)), ((), ())), preferred_element_type=jnp.float32)

    for t, (r, k) in enumerate(tiles):
        @pl.loop(0, 2)
        def _(half):
            part = pl.ds(pl.multiple_of(half * 256, 256), 256)
            ah, al = row_high[r], row_low[r]
            bh, bl = column_high[k, part, :], column_low[k, part, :]
            v = dot(ah, bh) + dot(ah, bl) + dot(al, bh)
            to = pl.ds(pl.multiple_of(before + t * TILE + half * 256, 256), 256)
            mine[:, to] = v[:256]
            other[:, to] = v[256:]


def products(place_now, tiles, rows, columns, before=()):
    start = before[0].shape[1] if before else 0
    arrays = []

    def index_of(chunk):
        for i, known in enumerate(arrays):
            if known is chunk:
                return i
        arrays.append(chunk)
        return len(arrays) - 1

    number = lambda pair: tuple(tuple(index_of(chunk) for chunk in block) for block in pair)
    rows, columns = [number(pair) for pair in rows], [number(pair) for pair in columns]
    width = start + TILE * len(tiles)
    operand = lambda n: pltpu.VMEM((n, TILE, 1024), jnp.bfloat16)
    return call(
        functools.partial(products_kernel, tiles, rows, columns, len(arrays), start),
        [(256, width)] * 2,
        [place_now, *arrays, *before],
        28,
        [operand(len(rows)), operand(len(rows)), operand(len(columns)), operand(len(columns))],
    )


def cores_kernel(place_ref, mine, got, *outs):
    for r in range(NY):
        rows = pl.ds(r * 64, 64)
        outs[r][...] = mine[rows, :] + got[rows, :]


def ys_kernel(place_ref, kept, a, b, d, mine, other):
    low, high = pl.ds(0, SHARE), pl.ds(SHARE, SHARE)
    mine[...] = kept[low, :] + a[low, :] + b[low, :] + d[low, :]
    other[...] = kept[high, :] + a[high, :] + b[high, :] + d[high, :]


def over_cores(place_now, mine, other):
    return call(cores_kernel, [(64, mine.shape[1])] * NY, [place_now, mine, send(other, swap_core)], 10)


def over_y(place_now, parts):
    got = [send(parts[r], y_by(r)) for r in (1, 3, 2)]
    return call(ys_kernel, [(SHARE, parts[0].shape[1])] * 2, [place_now, parts[0], *got], 4)


def over_x(mine, other):
    return mine + send(other, lambda y, xl, c, z, xh: (y, 1 - xl, c, z, xh))


def body(factors):
    aux, bas = lax.axis_index("aux"), lax.axis_index("bas")
    first = bas % 2 == 0
    place_now = jnp.stack([aux // 4, (aux // 2) % 2, aux % 2, bas % 2]).astype(jnp.int32)
    tie = lax.optimization_barrier
    same = lambda block: (tuple(block), tuple(block))

    own = factors[0]
    halves = own[:256], own[256:]
    o0 = send(own, swap_xh)
    p1 = [send(v, z_by(-1)) for v in halves]
    m1 = [send(v, z_by(1)) for v in halves]
    p1[1], m1[1], o0 = tie((p1[1], m1[1], o0))
    p2 = [send(v, z_by(-1)) for v in p1]
    m2 = [send(v, z_by(1)) for v in m1]

    product1 = products(
        place_now, [(0, 0), (0, 1), (1, 1), (1, 2)], [same([own]), same(m1)], [same([own]), same(p1), same([o0])]
    )
    p2[0], m2[0], product1 = tie((p2[0], m2[0], product1))
    o2 = [send(p2[0], swap_xh)]
    parts1 = over_cores(place_now, *product1)
    p2[1], m2, o2, parts1 = tie((p2[1], m2, o2, parts1))
    o2.append(send(p2[1], swap_xh))
    sums1 = over_y(place_now, parts1)
    product2 = products(place_now, [(0, 0), (0, 1), (0, 2)], [same(m2)], [same(p1), same(p2), same([o0])])
    o2, product2 = tie((o2, product2))
    product2 = products(
        place_now, [(0, 0), (1, 1)], [same(m1), ((own,), tuple(m2))], [same(o2), ((o0,), tuple(o2))], product2
    )
    product2, sums1 = tie((product2, sums1))
    parts2 = over_cores(place_now, *product2)

    v = over_x(*sums1)
    d0, d1, d2, t1 = jnp.split(v, 4, 1)
    d2, t1 = jnp.split(send(v[:, 1024:], z_by(-1)), 2, 1)
    v = over_x(*over_y(place_now, parts2))
    t3 = send(v[:, 1536:2048], z_by(-1))
    x = v[:, 2048:]
    d3, d4, t2, far = jnp.split(send(jnp.concatenate([v[:, :1536], x], 1), z_by(-2)), 4, 1)
    x = jnp.where(first, x, far)

    odd = [jnp.where(first, a, b) for a, b in ((x, t1), (t1, t2), (t2, t3), (t3, x))]
    return jnp.stack([d0, odd[0], d1, odd[1], d2, odd[2], d3, odd[3], d4], axis=1)[None]


def solution(mesh):
    return jax.shard_map(
        body,
        mesh=mesh,
        in_specs=(P("aux", "bas", None),),
        out_specs=P("bas", "aux", None, None),
        check_vma=False,
    )
```

time: 635 us -> 213 us (0.34)
  waiting for transfers between devices: 524 us -> 143 us
  Pallas kernels: 0 us -> 34.5 us
  matrix products: 32.6 us -> 0 us
  local copies, waits for them, and re-layouts: 22.7 us -> 3.61 us
  between operations: 13.5 us -> 0.2 us
  starting transfers between devices: 41.9 us -> 31 us
    ppermute x8 -> x24, waiting for transfers between devices: 334 us -> 143 us  [send(): return lax.ppermute(value, ('aux', 'bas'), pairs)]
    reduce_scatter x1 -> x0, waiting for transfers between devices: 190 us -> none  [body(): lax.psum_scatter(partial_value, 'aux', scatter_dimension=0, tiled=True)]
    pallas_call x0 -> x7, Pallas kernels: none -> 34.5 us  [call(): pl.pallas_call(kernel, out_shape=[jax.ShapeDtypeStruct(shape, jnp.float32...]
    dot_general x1 -> x0, matrix products: 32.6 us -> none  [products(): lax.dot_general(own_rows, stacked, (((0, 2), (1, 3)), ((), ())), precisio...]
    dot_general x1 -> x0, local copies, waits for them, and re-layouts: 16.7 us -> none  [products(): lax.dot_general(own_rows, stacked, (((0, 2), (1, 3)), ((), ())), precisio...]
    ppermute x8 -> x24, starting transfers between devices: 41.9 us -> 31 us  [send(): return lax.ppermute(value, ('aux', 'bas'), pairs)]
  transfers between devices with their start and end apart: 9 -> 24, of which waited for: 9 -> 19; matrix products, arithmetic and copies ran while one was open for 1% -> 1% of each run, Pallas kernels for 0% -> 12%
where the time goes in v1:
time: 213 us; the launch traced here: 212 us
  waiting for transfers between devices  143 us (67%)
  Pallas kernels  34.5 us (16%)
  starting transfers between devices  31 us (15%)
  local copies, waits for them, and re-layouts  3.61 us (2%)
    ppermute x24, waiting for transfers between devices, send(): return lax.ppermute(value, ('aux', 'bas'), pairs)  143 us
    pallas_call x7, Pallas kernels, call(): pl.pallas_call(kernel, out_shape=[jax.ShapeDtypeStruct(shape, jnp.float32...  34.5 us
    ppermute x24, starting transfers between devices, send(): return lax.ppermute(value, ('aux', 'bas'), pairs)  31 us
  transfers between devices with their start and end apart: 24, of which 19 were waited for; matrix products, arithmetic and copies ran while one was open for 1% of the time, Pallas kernels for 12%

profile of v1, /device:TPU:4, one launch (start us, length us, event | category | flops | bytes accessed | tf_op | source)
XLA Modules:
  0.0 212.1 jit_solution(9377110066638645248)
XLA Ops:
  0.0 2.2 %collective-permute-start.3 = (f32[512,1024]{1,0:T(8,128)}, f32[512,1024]{1,0:T(8,128)}, u32[]{:S(2)}, u32[]{:S(2)}) collective-permute-start(f32[512,1024]{1,0:T(8,128)} %bitcast.38), channel_id=1, source_target_pairs={{0,1},{1,0},{2,3},{3,2},{4,5},{5,4},{6,7},{7,6},{8,9},{9,8},{10,11... | collective-permute-start | bytes 6291464 | tf_op jit(solution)/shard_map/ppermute | solution.py:29
  2.2 2.7 %slice_bitcast_fusion = (f32[256,1024]{1,0:T(8,128)}, f32[256,1024]{1,0:T(8,128)S(1)}) fusion(f32[1,512,1024]{2,1,0:T(8,128)} %param.1), kind=kLoop, calls=%fused_computation | loop fusion | bytes 4194304 | tf_op jit(solution)/shard_map/slice | solution.py:175
  5.0 4.2 %collective-permute-start.5 = (f32[256,1024]{1,0:T(8,128)S(1)}, f32[256,1024]{1,0:T(8,128)S(1)}, u32[]{:S(2)}, u32[]{:S(2)}) collective-permute-start(f32[256,1024]{1,0:T(8,128)S(1)} %get-tuple-element.88), channel_id=1, source_target_pairs={{0,14},{1,15},{2,0},{3,1},{4,2},{5,3},{6,4},{7,5},{8,6},{9,7},{10,... | collective-permute-start | bytes 3145736 | tf_op jit(solution)/shard_map/ppermute | solution.py:29
  9.2 3.2 %collective-permute-start.1 = (f32[256,1024]{1,0:T(8,128)}, f32[256,1024]{1,0:T(8,128)}, u32[]{:S(2)}, u32[]{:S(2)}) collective-permute-start(f32[256,1024]{1,0:T(8,128)} %get-tuple-element.87), channel_id=1, source_target_pairs={{0,14},{1,15},{2,0},{3,1},{4,2},{5,3},{6,4},{7,5},{8,6},{9,7},{10,... | collective-permute-start | bytes 3145736 | tf_op jit(solution)/shard_map/ppermute | solution.py:29
  12.5 20.4 %collective-permute-done.5.refs_3_.refs_2_ = f32[256,1024]{1,0:T(8,128)S(1)} collective-permute-done((f32[256,1024]{1,0:T(8,128)S(1)}, f32[256,1024]{1,0:T(8,128)S(1)}, u32[]{:S(2)}, u32[]{:S(2)}) %collective-permute-start.5) | collective-permute-done | bytes 1048608 | tf_op jit(solution)/shard_map/ppermute | solution.py:29
  32.8 3.7 %collective-permute-start.6 = (f32[256,1024]{1,0:T(8,128)S(1)}, f32[256,1024]{1,0:T(8,128)}, u32[]{:S(2)}, u32[]{:S(2)}) collective-permute-start(f32[256,1024]{1,0:T(8,128)S(1)} %collective-permute-done.5.refs_3_.refs_2_), channel_id=1, source_target_pairs={{0,14},{1,15},{2,0},{3,1},{4,2},{5,3},{6,4},{7,5},{8,6},{9,7},{10,... | collective-permute-start | bytes 3145736 | tf_op jit(solution)/shard_map/ppermute | solution.py:29
  36.5 0.1 collective-permute-done.refs_1_.refs_0_
  36.6 0.1 pad_add_fusion.place_ref
  36.7 18.7 %collective-permute-done.1.refs_4_.refs_3_ = f32[256,1024]{1,0:T(8,128)} collective-permute-done((f32[256,1024]{1,0:T(8,128)}, f32[256,1024]{1,0:T(8,128)}, u32[]{:S(2)}, u32[]{:S(2)}) %collective-permute-start.1) | collective-permute-done | bytes 1048608 | tf_op jit(solution)/shard_map/ppermute | solution.py:29
  55.4 3.7 %collective-permute-done.2.refs_2_.refs_1_ = f32[256,1024]{1,0:T(8,128)} collective-permute-done((f32[256,1024]{1,0:T(8,128)}, f32[256,1024]{1,0:T(8,128)}, u32[]{:S(2)}, u32[]{:S(2)}) %collective-permute-start.2) | collective-permute-done | bytes 1048608 | tf_op jit(solution)/shard_map/ppermute | solution.py:29
  59.1 12.8 %shard_map.17 = (f32[256,2048]{1,0:T(8,128)S(1)}, f32[256,2048]{1,0:T(8,128)S(1)}) custom-call(s32[4]{0:T(128)S(1)} %pad_add_fusion.place_ref, f32[512,1024]{1,0:T(8,128)S(1)} %bitcast.39, f32[256,1024]{1,0:T(8,128)} %collective-permute-done.refs_1_.refs_0_, f32[256,1024]{1,0:T(8,128)} %collective-permute-done.2.refs_2_.refs_1_, ...), custom_call_target="tpu_custom_call" | custom-call | tf_op jit(solution)/shard_map/pallas_call | solution.py:49
  71.9 4.4 %collective-permute-done.6.refs_4_ = f32[256,1024]{1,0:T(8,128)} collective-permute-done((f32[256,1024]{1,0:T(8,128)S(1)}, f32[256,1024]{1,0:T(8,128)}, u32[]{:S(2)}, u32[]{:S(2)}) %collective-permute-start.6) | collective-permute-done | bytes 1048608 | tf_op jit(solution)/shard_map/ppermute | solution.py:29
  76.3 3.5 %collective-permute-done.7.refs_0_.refs_3_ = f32[256,1024]{1,0:T(8,128)} collective-permute-done((f32[256,1024]{1,0:T(8,128)}, f32[256,1024]{1,0:T(8,128)}, u32[]{:S(2)}, u32[]{:S(2)}) %collective-permute-start.7) | collective-permute-done | bytes 1048608 | tf_op jit(solution)/shard_map/ppermute | solution.py:29
  79.8 2.9 %collective-permute-start.9 = (f32[256,1024]{1,0:T(8,128)}, f32[256,1024]{1,0:T(8,128)S(1)}, u32[]{:S(2)}, u32[]{:S(2)}) collective-permute-start(f32[256,1024]{1,0:T(8,128)} %collective-permute-done.6.refs_4_), channel_id=1, source_target_pairs={{0,1},{1,0},{2,3},{3,2},{4,5},{5,4},{6,7},{7,6},{8,9},{9,8},{10,11... | collective-permute-start | bytes 3145736 | tf_op jit(solution)/shard_map/ppermute | solution.py:29
  82.7 0.3 collective-permute-start.4
  83.0 1.7 collective-permute-start.8
  84.7 0.8 shard_map.18
  85.5 21.6 %collective-permute-done.9.refs_5_ = f32[256,1024]{1,0:T(8,128)S(1)} collective-permute-done((f32[256,1024]{1,0:T(8,128)}, f32[256,1024]{1,0:T(8,128)S(1)}, u32[]{:S(2)}, u32[]{:S(2)}) %collective-permute-start.9) | collective-permute-done | bytes 1048608 | tf_op jit(solution)/shard_map/ppermute | solution.py:29
  107.1 1.1 collective-permute-done.4.refs_5_
  108.2 1.2 collective-permute-done.8.refs_1_.refs_4_
  109.4 0.6 collective-permute-start.11
  110.1 1.6 collective-permute-start.12
  111.6 1.7 collective-permute-start.13
  113.3 2.0 collective-permute-start.14
  115.3 10.2 %shard_map.19 = (f32[256,1536]{1,0:T(8,128)S(1)}, f32[256,1536]{1,0:T(8,128)S(1)}) custom-call(s32[4]{0:T(128)S(1)} %pad_add_fusion.place_ref, f32[256,1024]{1,0:T(8,128)} %collective-permute-done.7.refs_0_.refs_3_, f32[256,1024]{1,0:T(8,128)S(1)} %collective-permute-done.8.refs_1_.refs_4_, f32[256,1024]{1,0:T(8,128)S(1)} %collective-permute-done.5.refs_3_.refs_2_, ...), custom_call_target="tpu_custom_call" | custom-call | tf_op jit(solution)/shard_map/pallas_call | solution.py:49
  125.5 1.0 collective-permute-done.13.b
  126.5 10.5 %collective-permute-done.14.d = f32[64,2048]{1,0:T(8,128)S(1)} collective-permute-done((f32[64,2048]{1,0:T(8,128)S(1)}, f32[64,2048]{1,0:T(8,128)S(1)}, u32[]{:S(2)}, u32[]{:S(2)}) %collective-permute-start.14) | collective-permute-done | bytes 524320 | tf_op jit(solution)/shard_map/ppermute | solution.py:29
  137.0 0.6 shard_map.21
  137.6 8.6 %shard_map.20 = (f32[256,2560]{1,0:T(8,128)S(1)}, f32[256,2560]{1,0:T(8,128)S(1)}) custom-call(s32[4]{0:T(128)S(1)} %pad_add_fusion.place_ref, f32[256,1024]{1,0:T(8,128)} %collective-permute-done.refs_1_.refs_0_, f32[256,1024]{1,0:T(8,128)} %collective-permute-done.2.refs_2_.refs_1_, f32[512,1024]{1,0:T(8,128)S(1)} %bitcast.40, ...), custom_call_target="tpu_custom_call" | custom-call | tf_op jit(solution)/shard_map/pallas_call | solution.py:49
  146.2 0.1 collective-permute-start.16
  146.3 4.9 %collective-permute-done.16.got = f32[256,2560]{1,0:T(8,128)S(1)} collective-permute-done((f32[256,2560]{1,0:T(8,128)S(1)}, f32[256,2560]{1,0:T(8,128)S(1)}, u32[]{:S(2)}, u32[]{:S(2)}) %collective-permute-start.16) | collective-permute-done | bytes 2621472 | tf_op jit(solution)/shard_map/ppermute | solution.py:29
  151.2 0.8 shard_map.22
  152.1 1.2 collective-permute-start.17
  153.3 2.1 collective-permute-start.18
  155.4 15.5 %collective-permute-done.17.a = f32[64,2560]{1,0:T(8,128)S(1)} collective-permute-done((f32[64,2560]{1,0:T(8,128)S(1)}, f32[64,2560]{1,0:T(8,128)S(1)}, u32[]{:S(2)}, u32[]{:S(2)}) %collective-permute-start.17) | collective-permute-done | bytes 655392 | tf_op jit(solution)/shard_map/ppermute | solution.py:29
  170.9 12.5 %collective-permute-done.18.b = f32[64,2560]{1,0:T(8,128)S(1)} collective-permute-done((f32[64,2560]{1,0:T(8,128)S(1)}, f32[64,2560]{1,0:T(8,128)S(1)}, u32[]{:S(2)}, u32[]{:S(2)}) %collective-permute-start.18) | collective-permute-done | bytes 655392 | tf_op jit(solution)/shard_map/ppermute | solution.py:29
  183.5 0.7 collective-permute-done.19.d
  184.2 0.7 shard_map.23
  184.8 1.5 collective-permute-start.20
  186.3 0.6 collective-permute-start.15
  186.9 8.6 %collective-permute-done.20 = f32[32,2560]{1,0:T(8,128)S(1)} collective-permute-done((f32[32,2560]{1,0:T(8,128)S(1)}, f32[32,2560]{1,0:T(8,128)S(1)}, u32[]{:S(2)}, u32[]{:S(2)}) %collective-permute-start.20) | collective-permute-done | bytes 327712 | tf_op jit(solution)/shard_map/ppermute | solution.py:29
  195.7 0.3 collective-permute-start.21
  196.0 3.5 %collective-permute-done.15 = f32[32,2048]{1,0:T(8,128)S(1)} collective-permute-done((f32[32,2048]{1,0:T(8,128)S(1)}, f32[32,2048]{1,0:T(8,128)S(1)}, u32[]{:S(2)}, u32[]{:S(2)}) %collective-permute-start.15) | collective-permute-done | bytes 262176 | tf_op jit(solution)/shard_map/ppermute | solution.py:29
  199.5 0.4 collective-permute-start.22
  199.9 0.5 collective-permute-start.23
  200.4 10.1 %collective-permute-done.22 = f32[32,1024]{1,0:T(8,128)S(1)} collective-permute-done((f32[32,1024]{1,0:T(8,128)S(1)}, f32[32,1024]{1,0:T(8,128)S(1)}, u32[]{:S(2)}, u32[]{:S(2)}) %collective-permute-start.22) | collective-permute-done | bytes 131104 | tf_op jit(solution)/shard_map/ppermute | solution.py:29
  210.6 0.6 collective-permute-done.23
  211.3 0.8 copy-done.1
  (28 shorter events, 0.3 us)
Async XLA Ops:
  0.0 59.1 %copy-start = (f32[1,512,1024]{2,1,0:T(8,128)S(1)}, f32[1,512,1024]{2,1,0:T(8,128)}, u32[]{:S(2)}) copy-start(f32[1,512,1024]{2,1,0:T(8,128)} %param.1) | copy-start | bytes 6291460
  0.0 59.1 %collective-permute-start.3 = (f32[512,1024]{1,0:T(8,128)}, f32[512,1024]{1,0:T(8,128)}, u32[]{:S(2)}, u32[]{:S(2)}) collective-permute-start(f32[512,1024]{1,0:T(8,128)} %bitcast.38), channel_id=1, source_target_pairs={{0,1},{1,0},{2,3},{3,2},{4,5},{5,4},{6,7},{7,6},{8,9},{9,8},{10,11... | collective-permute-start | bytes 6291464 | tf_op jit(solution)/shard_map/ppermute | solution.py:29
  5.0 27.8 %collective-permute-start.5 = (f32[256,1024]{1,0:T(8,128)S(1)}, f32[256,1024]{1,0:T(8,128)S(1)}, u32[]{:S(2)}, u32[]{:S(2)}) collective-permute-start(f32[256,1024]{1,0:T(8,128)S(1)} %get-tuple-element.88), channel_id=1, source_target_pairs={{0,14},{1,15},{2,0},{3,1},{4,2},{5,3},{6,4},{7,5},{8,6},{9,7},{10,... | collective-permute-start | bytes 3145736 | tf_op jit(solution)/shard_map/ppermute | solution.py:29
  9.2 27.4 %collective-permute-start = (f32[256,1024]{1,0:T(8,128)S(1)}, f32[256,1024]{1,0:T(8,128)}, u32[]{:S(2)}, u32[]{:S(2)}) collective-permute-start(f32[256,1024]{1,0:T(8,128)S(1)} %get-tuple-element.88), channel_id=1, source_target_pairs={{0,2},{1,3},{2,4},{3,5},{4,6},{5,7},{6,8},{7,9},{8,10},{9,11},{10,... | collective-permute-start | bytes 3145736 | tf_op jit(solution)/shard_map/ppermute | solution.py:29
  9.2 46.2 %collective-permute-start.1 = (f32[256,1024]{1,0:T(8,128)}, f32[256,1024]{1,0:T(8,128)}, u32[]{:S(2)}, u32[]{:S(2)}) collective-permute-start(f32[256,1024]{1,0:T(8,128)} %get-tuple-element.87), channel_id=1, source_target_pairs={{0,14},{1,15},{2,0},{3,1},{4,2},{5,3},{6,4},{7,5},{8,6},{9,7},{10,... | collective-permute-start | bytes 3145736 | tf_op jit(solution)/shard_map/ppermute | solution.py:29
  12.5 46.6 %collective-permute-start.2 = (f32[256,1024]{1,0:T(8,128)}, f32[256,1024]{1,0:T(8,128)}, u32[]{:S(2)}, u32[]{:S(2)}) collective-permute-start(f32[256,1024]{1,0:T(8,128)} %get-tuple-element.87), channel_id=1, source_target_pairs={{0,2},{1,3},{2,4},{3,5},{4,6},{5,7},{6,8},{7,9},{8,10},{9,11},{10,... | collective-permute-start | bytes 3145736 | tf_op jit(solution)/shard_map/ppermute | solution.py:29
  32.8 43.5 %collective-permute-start.6 = (f32[256,1024]{1,0:T(8,128)S(1)}, f32[256,1024]{1,0:T(8,128)}, u32[]{:S(2)}, u32[]{:S(2)}) collective-permute-start(f32[256,1024]{1,0:T(8,128)S(1)} %collective-permute-done.5.refs_3_.refs_2_), channel_id=1, source_target_pairs={{0,14},{1,15},{2,0},{3,1},{4,2},{5,3},{6,4},{7,5},{8,6},{9,7},{10,... | collective-permute-start | bytes 3145736 | tf_op jit(solution)/shard_map/ppermute | solution.py:29
  36.6 43.2 %collective-permute-start.7 = (f32[256,1024]{1,0:T(8,128)}, f32[256,1024]{1,0:T(8,128)}, u32[]{:S(2)}, u32[]{:S(2)}) collective-permute-start(f32[256,1024]{1,0:T(8,128)} %collective-permute-done.refs_1_.refs_0_), channel_id=1, source_target_pairs={{0,2},{1,3},{2,4},{3,5},{4,6},{5,7},{6,8},{7,9},{8,10},{9,11},{10,... | collective-permute-start | bytes 3145736 | tf_op jit(solution)/shard_map/ppermute | solution.py:29
  79.8 4.9 %collective-permute-start.10 = (f32[256,2048]{1,0:T(8,128)S(1)}, f32[256,2048]{1,0:T(8,128)S(1)}, u32[]{:S(2)}, u32[]{:S(2)}) collective-permute-start(f32[256,2048]{1,0:T(8,128)S(1)} %get-tuple-element.54), channel_id=1, source_target_pairs={{0,16},{1,17},{2,18},{3,19},{4,20},{5,21},{6,22},{7,23},{8,24},{9,... | collective-permute-start | bytes 6291464 | tf_op jit(solution)/shard_map/ppermute | solution.py:29
  79.8 27.3 %collective-permute-start.9 = (f32[256,1024]{1,0:T(8,128)}, f32[256,1024]{1,0:T(8,128)S(1)}, u32[]{:S(2)}, u32[]{:S(2)}) collective-permute-start(f32[256,1024]{1,0:T(8,128)} %collective-permute-done.6.refs_4_), channel_id=1, source_target_pairs={{0,1},{1,0},{2,3},{3,2},{4,5},{5,4},{6,7},{7,6},{8,9},{9,8},{10,11... | collective-permute-start | bytes 3145736 | tf_op jit(solution)/shard_map/ppermute | solution.py:29
  82.7 25.5 %collective-permute-start.4 = (f32[256,1024]{1,0:T(8,128)}, f32[256,1024]{1,0:T(8,128)S(1)}, u32[]{:S(2)}, u32[]{:S(2)}) collective-permute-start(f32[256,1024]{1,0:T(8,128)} %collective-permute-done.1.refs_4_.refs_3_), channel_id=1, source_target_pairs={{0,14},{1,15},{2,0},{3,1},{4,2},{5,3},{6,4},{7,5},{8,6},{9,7},{10,... | collective-permute-start | bytes 3145736 | tf_op jit(solution)/shard_map/ppermute | solution.py:29
  83.0 26.4 %collective-permute-start.8 = (f32[256,1024]{1,0:T(8,128)}, f32[256,1024]{1,0:T(8,128)S(1)}, u32[]{:S(2)}, u32[]{:S(2)}) collective-permute-start(f32[256,1024]{1,0:T(8,128)} %collective-permute-done.2.refs_2_.refs_1_), channel_id=1, source_target_pairs={{0,2},{1,3},{2,4},{3,5},{4,6},{5,7},{6,8},{7,9},{8,10},{9,11},{10,... | collective-permute-start | bytes 3145736 | tf_op jit(solution)/shard_map/ppermute | solution.py:29
  109.4 28.2 %collective-permute-start.11 = (f32[256,1024]{1,0:T(8,128)S(1)}, f32[256,1024]{1,0:T(8,128)S(1)}, u32[]{:S(2)}, u32[]{:S(2)}) collective-permute-start(f32[256,1024]{1,0:T(8,128)S(1)} %collective-permute-done.4.refs_5_), channel_id=1, source_target_pairs={{0,1},{1,0},{2,3},{3,2},{4,5},{5,4},{6,7},{7,6},{8,9},{9,8},{10,11... | collective-permute-start | bytes 3145736 | tf_op jit(solution)/shard_map/ppermute | solution.py:29
  110.1 15.5 %collective-permute-start.12 = (f32[64,2048]{1,0:T(8,128)S(1)}, f32[64,2048]{1,0:T(8,128)S(1)}, u32[]{:S(2)}, u32[]{:S(2)}) collective-permute-start(f32[64,2048]{1,0:T(8,128)S(1)} %get-tuple-element.72), channel_id=1, source_target_pairs={{0,64},{1,65},{2,66},{3,67},{4,68},{5,69},{6,70},{7,71},{8,72},{9,... | collective-permute-start | bytes 1572872 | tf_op jit(solution)/shard_map/ppermute | solution.py:29
  111.6 14.9 %collective-permute-start.13 = (f32[64,2048]{1,0:T(8,128)S(1)}, f32[64,2048]{1,0:T(8,128)S(1)}, u32[]{:S(2)}, u32[]{:S(2)}) collective-permute-start(f32[64,2048]{1,0:T(8,128)S(1)} %get-tuple-element.73), channel_id=1, source_target_pairs={{0,192},{1,193},{2,194},{3,195},{4,196},{5,197},{6,198},{7,199},{8... | collective-permute-start | bytes 1572872 | tf_op jit(solution)/shard_map/ppermute | solution.py:29
  113.3 23.7 %collective-permute-start.14 = (f32[64,2048]{1,0:T(8,128)S(1)}, f32[64,2048]{1,0:T(8,128)S(1)}, u32[]{:S(2)}, u32[]{:S(2)}) collective-permute-start(f32[64,2048]{1,0:T(8,128)S(1)} %get-tuple-element.74), channel_id=1, source_target_pairs={{0,128},{1,129},{2,130},{3,131},{4,132},{5,133},{6,134},{7,135},{8... | collective-permute-start | bytes 1572872 | tf_op jit(solution)/shard_map/ppermute | solution.py:29
  146.2 5.0 %collective-permute-start.16 = (f32[256,2560]{1,0:T(8,128)S(1)}, f32[256,2560]{1,0:T(8,128)S(1)}, u32[]{:S(2)}, u32[]{:S(2)}) collective-permute-start(f32[256,2560]{1,0:T(8,128)S(1)} %get-tuple-element.80), channel_id=1, source_target_pairs={{0,16},{1,17},{2,18},{3,19},{4,20},{5,21},{6,22},{7,23},{8,24},{9,... | collective-permute-start | bytes 7864328 | tf_op jit(solution)/shard_map/ppermute | solution.py:29
  152.1 18.9 %collective-permute-start.17 = (f32[64,2560]{1,0:T(8,128)S(1)}, f32[64,2560]{1,0:T(8,128)S(1)}, u32[]{:S(2)}, u32[]{:S(2)}) collective-permute-start(f32[64,2560]{1,0:T(8,128)S(1)} %get-tuple-element.82), channel_id=1, source_target_pairs={{0,64},{1,65},{2,66},{3,67},{4,68},{5,69},{6,70},{7,71},{8,72},{9,... | collective-permute-start | bytes 1966088 | tf_op jit(solution)/shard_map/ppermute | solution.py:29
  153.3 30.2 %collective-permute-start.18 = (f32[64,2560]{1,0:T(8,128)S(1)}, f32[64,2560]{1,0:T(8,128)S(1)}, u32[]{:S(2)}, u32[]{:S(2)}) collective-permute-start(f32[64,2560]{1,0:T(8,128)S(1)} %get-tuple-element.83), channel_id=1, source_target_pairs={{0,192},{1,193},{2,194},{3,195},{4,196},{5,197},{6,198},{7,199},{8... | collective-permute-start | bytes 1966088 | tf_op jit(solution)/shard_map/ppermute | solution.py:29
  155.4 28.8 %collective-permute-start.19 = (f32[64,2560]{1,0:T(8,128)S(1)}, f32[64,2560]{1,0:T(8,128)S(1)}, u32[]{:S(2)}, u32[]{:S(2)}) collective-permute-start(f32[64,2560]{1,0:T(8,128)S(1)} %get-tuple-element.84), channel_id=1, source_target_pairs={{0,128},{1,129},{2,130},{3,131},{4,132},{5,133},{6,134},{7,135},{8... | collective-permute-start | bytes 1966088 | tf_op jit(solution)/shard_map/ppermute | solution.py:29
  184.8 10.7 %collective-permute-start.20 = (f32[32,2560]{1,0:T(8,128)S(1)}, f32[32,2560]{1,0:T(8,128)S(1)}, u32[]{:S(2)}, u32[]{:S(2)}) collective-permute-start(f32[32,2560]{1,0:T(8,128)S(1)} %get-tuple-element.86), channel_id=1, source_target_pairs={{0,32},{1,33},{2,34},{3,35},{4,36},{5,37},{6,38},{7,39},{8,40},{9,... | collective-permute-start | bytes 983048 | tf_op jit(solution)/shard_map/ppermute | solution.py:29
  186.3 13.2 %collective-permute-start.15 = (f32[32,2048]{1,0:T(8,128)S(1)}, f32[32,2048]{1,0:T(8,128)S(1)}, u32[]{:S(2)}, u32[]{:S(2)}) collective-permute-start(f32[32,2048]{1,0:T(8,128)S(1)} %get-tuple-element.78), channel_id=1, source_target_pairs={{0,32},{1,33},{2,34},{3,35},{4,36},{5,37},{6,38},{7,39},{8,40},{9,... | collective-permute-start | bytes 786440 | tf_op jit(solution)/shard_map/ppermute | solution.py:29
  195.7 14.8 %collective-permute-start.21 = (f32[32,2048]{1,0:T(8,128)S(1)}, f32[32,2048]{1,0:T(8,128)S(1)}, u32[]{:S(2)}, u32[]{:S(2)}) collective-permute-start(f32[32,2048]{1,0:T(8,128)S(1)} %pad_maximum_fusion), channel_id=1, source_target_pairs={{0,12},{1,13},{2,14},{3,15},{4,0},{5,1},{6,2},{7,3},{8,4},{9,5},{1... | collective-permute-start | bytes 786440 | tf_op jit(solution)/shard_map/ppermute | solution.py:29
  199.5 11.0 %collective-permute-start.22 = (f32[32,1024]{1,0:T(8,128)S(1)}, f32[32,1024]{1,0:T(8,128)S(1)}, u32[]{:S(2)}, u32[]{:S(2)}) collective-permute-start(f32[32,1024]{1,0:T(8,128)S(1)} %slice.34), channel_id=1, source_target_pairs={{0,14},{1,15},{2,0},{3,1},{4,2},{5,3},{6,4},{7,5},{8,6},{9,7},{10,... | collective-permute-start | bytes 393224 | tf_op jit(solution)/shard_map/ppermute | solution.py:29
  199.9 11.4 %collective-permute-start.23 = (f32[32,512]{1,0:T(8,128)S(1)}, f32[32,512]{1,0:T(8,128)S(1)}, u32[]{:S(2)}, u32[]{:S(2)}) collective-permute-start(f32[32,512]{1,0:T(8,128)S(1)} %get-tuple-element.89), channel_id=1, source_target_pairs={{0,14},{1,15},{2,0},{3,1},{4,2},{5,3},{6,4},{7,5},{8,6},{9,7},{10,... | collective-permute-start | bytes 196616 | tf_op jit(solution)/shard_map/ppermute | solution.py:29
  211.3 0.8 copy-start.1

commit v2 on v1

v2 whole, which is shorter than its diff:
```python
import functools

import jax
import jax.numpy as jnp
from jax import lax
from jax.experimental import pallas as pl
from jax.experimental.pallas import tpu as pltpu
from jax.sharding import PartitionSpec as P

NY, NXL, NC, NZ, NXH = 4, 2, 2, 8, 2
TILE = 512
SHARE = 32
HEAD = 192


def place(y, xl, c, z, xh):
    return (((y % NY) * NXL + xl % NXL) * NC + c % NC) * (NZ * NXH) + (z % NZ) * NXH + xh % NXH


def send(value, target):
    pairs = []
    for y in range(NY):
        for xl in range(NXL):
            for c in range(NC):
                for z in range(NZ):
                    for xh in range(NXH):
                        to = target(y, xl, c, z, xh)
                        if to is not None:
                            pairs.append((place(y, xl, c, z, xh), place(*to)))
    return lax.ppermute(value, ("aux", "bas"), pairs)


def z_by(step):
    return lambda y, xl, c, z, xh: (y, xl, c, z + step, xh)


def y_by(step):
    return lambda y, xl, c, z, xh: (y + step, xl, c, z, xh)


def swap_core(y, xl, c, z, xh):
    return y, xl, 1 - c, z, xh


def swap_xl(y, xl, c, z, xh):
    return y, 1 - xl, c, z, xh


def swap_xh(y, xl, c, z, xh):
    return y, xl, c, z, 1 - xh


def call(kernel, outs, args, vmem, dtype=jnp.float32):
    return pl.pallas_call(
        kernel,
        out_shape=[jax.ShapeDtypeStruct(shape, dtype) for shape in outs],
        in_specs=[pl.BlockSpec(memory_space=pltpu.SMEM)] + [pl.BlockSpec(memory_space=pltpu.VMEM)] * (len(args) - 1),
        out_specs=[pl.BlockSpec(memory_space=pltpu.VMEM)] * len(outs),
        compiler_params=pltpu.CompilerParams(vmem_limit_bytes=vmem * 2**20),
        cost_estimate=pl.CostEstimate(flops=0, bytes_accessed=0, transcendentals=0),
    )(*args)


def two_terms(value):
    high = value.astype(jnp.bfloat16)
    return high, (value - high.astype(jnp.float32)).astype(jnp.bfloat16)


def split_kernel(rows, columns, count, place_ref, *refs):
    operands, outs = refs[:count], refs[count:]
    y, xl, c, xh = (place_ref[i] for i in range(4))

    def split(block, high, low, target):
        done = 0
        for at, first in block:
            chunk = operands[at]
            groups = chunk.shape[0] // SHARE
            depth = high.shape[1]

            @pl.loop(0, groups)
            def _(g, chunk=chunk, done=done, first=first, depth=depth):
                to = pl.ds(pl.multiple_of(target(g + done) * SHARE, SHARE), SHARE)
                value = chunk[pl.ds(pl.multiple_of(g * SHARE, SHARE), SHARE), first:first + depth]
                high[to, :], low[to, :] = two_terms(value)

            done += groups

    def row_target(g):
        return (g % 2 + 2 - c) % 2 * 8 + (g // 4 + 4 - y) % 4 * 2 + (g // 2 % 2 + 2 - xl) % 2

    for i, pair in enumerate(rows + columns):
        target = row_target if i < len(rows) else lambda g: g
        high, low = outs[2 * i], outs[2 * i + 1]
        if pair[0] == pair[1]:
            split(pair[0], high, low, target)
        else:
            for column_of_chips in range(2):
                @pl.when(xh == column_of_chips)
                def _():
                    split(pair[column_of_chips], high, low, target)


def split(place_now, rows, columns, depth=1024):
    arrays = []

    def index_of(chunk):
        for i, known in enumerate(arrays):
            if known is chunk:
                return i
        arrays.append(chunk)
        return len(arrays) - 1

    number = lambda pair: tuple(tuple((index_of(chunk), first) for chunk, first in block) for block in pair)
    rows, columns = [number(pair) for pair in rows], [number(pair) for pair in columns]
    outs = call(
        functools.partial(split_kernel, rows, columns, len(arrays)),
        [(TILE, depth)] * (2 * len(rows + columns)),
        [place_now, *arrays],
        24,
        jnp.bfloat16,
    )
    return [tuple(outs[i:i + 2]) for i in range(0, len(outs), 2)]


def products_kernel(tiles, either, count, before, place_ref, *refs):
    operands, (mine, other) = refs[:count], refs[-2:]
    if before:
        mine[:, :before] = refs[count][...]
        other[:, :before] = refs[count + 1][...]

    def dot(a, b):
        return lax.dot_general(a, b, (((1,), (1,)), ((), ())), preferred_element_type=jnp.float32)

    def write(t, tile):
        rh, rl, ch, cl = tile

        @pl.loop(0, 2)
        def _(half):
            part = pl.ds(pl.multiple_of(half * 256, 256), 256)
            ah, al = operands[rh][...], operands[rl][...]
            bh, bl = operands[ch][part, :], operands[cl][part, :]
            v = dot(ah, bh) + dot(ah, bl) + dot(al, bh)
            to = pl.ds(pl.multiple_of(before + t * TILE + half * 256, 256), 256)
            mine[:, to] = v[:256]
            other[:, to] = v[256:]

    for t, tile in enumerate(tiles):
        write(t, tile)
    for column_of_chips, tile in enumerate(either):
        @pl.when(place_ref[3] == column_of_chips)
        def _():
            write(len(tiles), tile)


def products(place_now, pairs, before=(), either=()):
    arrays = []

    def index_of(array):
        for i, known in enumerate(arrays):
            if known is array:
                return i
        arrays.append(array)
        return len(arrays) - 1

    number = lambda some: [tuple(index_of(array) for array in rows + columns) for rows, columns in some]
    tiles, either = number(pairs), number(either)
    start = before[0].shape[1] if before else 0
    width = start + TILE * (len(tiles) + bool(either))
    kernel = functools.partial(products_kernel, tiles, either, len(arrays), start)
    return call(kernel, [(256, width)] * 2, [place_now, *arrays, *before], 28)


def cores_kernel(place_ref, mine, got, *outs):
    for r in range(NY):
        rows = pl.ds(r * 64, 64)
        outs[r][...] = mine[rows, :] + got[rows, :]


def ys_kernel(place_ref, kept, a, b, d, mine, other):
    low, high = pl.ds(0, SHARE), pl.ds(SHARE, SHARE)
    mine[...] = kept[low, :] + a[low, :] + b[low, :] + d[low, :]
    other[...] = kept[high, :] + a[high, :] + b[high, :] + d[high, :]


def over_cores(place_now, mine, other):
    return call(cores_kernel, [(64, mine.shape[1])] * NY, [place_now, mine, send(other, swap_core)], 10)


def mixed_cores_kernel(width, place_ref, mine, got, *outs):
    by_y, by_x = outs[:NY], outs[NY:]
    for r in range(NY):
        rows = pl.ds(r * 64, 64)
        by_y[r][...] = mine[rows, :width] + got[rows, :width]
        for x in range(NXL):
            rows = pl.ds(r * 64 + x * SHARE, SHARE)
            by_x[x][pl.ds(r * SHARE, SHARE), :] = mine[rows, width:] + got[rows, width:]


def mixed_kernel(place_ref, kept, a, b, d, kept_x, got_x, mine, other, *outs):
    ys_kernel(place_ref, kept, a, b, d, mine, other)
    for r in range(NY):
        rows = pl.ds(r * SHARE, SHARE)
        outs[r][...] = kept_x[rows, :] + got_x[rows, :]


def mixed_sum(place_now, mine, other, width):
    rest = mine.shape[1] - width
    shapes = [(64, width)] * NY + [(NY * SHARE, rest)] * NXL
    outs = call(functools.partial(mixed_cores_kernel, width), shapes, [place_now, mine, send(other, swap_core)], 12)
    by_y, by_x = outs[:NY], outs[NY:]
    got = [send(by_y[r], y_by(r)) for r in (1, 3, 2)] + [by_x[0], send(by_x[1], swap_xl)]
    shapes = [(SHARE, width)] * 2 + [(SHARE, rest)] * NY
    mine, other, *by_y = call(mixed_kernel, shapes, [place_now, by_y[0], *got], 8)
    got = [send(by_y[r], y_by(r)) for r in (1, 3, 2)]
    return mine + send(other, swap_xl), by_y[0] + got[0] + got[1] + got[2]


def over_y(place_now, parts):
    got = [send(parts[r], y_by(r)) for r in (1, 3, 2)]
    return call(ys_kernel, [(SHARE, parts[0].shape[1])] * 2, [place_now, parts[0], *got], 4)


def over_x(mine, other):
    return mine + send(other, swap_xl)


def body(factors):
    aux, bas = lax.axis_index("aux"), lax.axis_index("bas")
    first = bas % 2 == 0
    place_now = jnp.stack([aux // 4, aux // 2 % 2, aux % 2, bas % 2]).astype(jnp.int32)
    tie = lax.optimization_barrier
    whole = lambda *chunks: (tuple((chunk, 0) for chunk in chunks),) * 2

    own = factors[0]
    rows_own, cols_own = split(place_now, [whole(own)], [whole(own)])
    p1, m1, o0 = send(own, z_by(-1)), send(own, z_by(1)), send(own, swap_xh)
    p1, m1, o0, rows_own, cols_own = tie((p1, m1, o0, rows_own, cols_own))

    p1a, p1b, m1a, m1b = p1[:HEAD], p1[HEAD:], m1[:HEAD], m1[HEAD:]
    p2a, m2a = send(p1a, z_by(-1)), send(m1a, z_by(1))
    rows_m1, cols_p1, cols_o0 = split(place_now, [whole(m1)], [whole(p1), whole(o0)])
    product1 = products(
        place_now, [(rows_own, cols_own), (rows_own, cols_p1), (rows_m1, cols_p1), (rows_m1, cols_o0)]
    )
    p2a, m2a, product1, p1b, m1b = tie((p2a, m2a, product1, p1b, m1b))

    p2b, m2b, o2a = send(p1b, z_by(-1)), send(m1b, z_by(1)), send(p2a, swap_xh)
    parts1 = over_cores(place_now, *product1)
    p2b, m2b, o2a, parts1 = tie((p2b, m2b, o2a, parts1))

    o2b = send(p2b, swap_xh)
    sums1 = over_y(place_now, parts1)
    rows_m2, cols_p2 = split(place_now, [whole(m2a, m2b)], [whole(p2a, p2b)])
    product2 = products(place_now, [(rows_m2, cols) for cols in (cols_p1, cols_p2, cols_o0)])
    o2b, product2 = tie((o2b, product2))
    o2 = ((o2a, 0), (o2b, 0))
    (cols_o2,) = split(place_now, [], [(o2, o2)])
    product2 = products(place_now, [(rows_m1, cols_o2)], product2, ((rows_own, cols_o0), (rows_m2, cols_o2)))
    product2, sums1 = tie((product2, sums1))
    far, v = mixed_sum(place_now, *product2, 1536)
    d3, d4, t2 = jnp.split(send(far, z_by(-2)), 3, 1)
    t3, x = send(v[:, :512], z_by(-1)), v[:, 512:]
    x = jnp.where(first, x, send(x, z_by(-2)))

    v = over_x(*sums1)
    d0, d1 = jnp.split(v[:, :1024], 2, 1)
    d2, t1 = jnp.split(send(v[:, 1024:], z_by(-1)), 2, 1)

    odd = [jnp.where(first, a, b) for a, b in ((x, t1), (t1, t2), (t2, t3), (t3, x))]
    return jnp.stack([d0, odd[0], d1, odd[1], d2, odd[2], d3, odd[3], d4], axis=1)[None]


def solution(mesh):
    return jax.shard_map(
        body,
        mesh=mesh,
        in_specs=(P("aux", "bas", None),),
        out_specs=P("bas", "aux", None, None),
        check_vma=False,
    )
```

time: 213 us -> 202 us (0.948)
  waiting for transfers between devices: 143 us -> 133 us
  Pallas kernels: 34.5 us -> 30.2 us
    ppermute x24 -> x27, waiting for transfers between devices: 143 us -> 133 us  [send(): return lax.ppermute(value, ('aux', 'bas'), pairs)]
    pallas_call x7 -> x11, Pallas kernels: 34.5 us -> 30.2 us  [call(): pl.pallas_call(kernel, out_shape=[jax.ShapeDtypeStruct(shape, dtype) for...]
    ppermute x24 -> x27, starting transfers between devices: 31 us -> 32.9 us  [send(): return lax.ppermute(value, ('aux', 'bas'), pairs)]
  transfers between devices with their start and end apart: 24 -> 27, of which waited for: 19 -> 22; matrix products, arithmetic and copies ran while one was open for 1% -> 1% of each run, Pallas kernels for 12% -> 12%
where the time goes in v2:
time: 202 us
  waiting for transfers between devices  133 us (66%)
  starting transfers between devices  32.9 us (16%)
  Pallas kernels  30.2 us (15%)
  local copies, waits for them, and re-layouts  5.19 us (3%)
    ppermute x27, waiting for transfers between devices, send(): return lax.ppermute(value, ('aux', 'bas'), pairs)  133 us
    ppermute x27, starting transfers between devices, send(): return lax.ppermute(value, ('aux', 'bas'), pairs)  32.9 us
    pallas_call x11, Pallas kernels, call(): pl.pallas_call(kernel, out_shape=[jax.ShapeDtypeStruct(shape, dtype) for...  30.2 us
  transfers between devices with their start and end apart: 27, of which 22 were waited for; matrix products, arithmetic and copies ran while one was open for 1% of the time, Pallas kernels for 12%

profile of v2, /device:TPU:4, one launch (start us, length us, event | category | flops | bytes accessed | tf_op | source)
XLA Modules:
  0.0 201.7 jit_solution(9795468392771919188)
XLA Ops:
  0.0 5.9 %collective-permute-start = (f32[512,1024]{1,0:T(8,128)}, f32[512,1024]{1,0:T(8,128)S(1)}, u32[]{:S(2)}, u32[]{:S(2)}) collective-permute-start(f32[512,1024]{1,0:T(8,128)} %bitcast.34), channel_id=1, source_target_pairs={{0,14},{1,15},{2,0},{3,1},{4,2},{5,3},{6,4},{7,5},{8,6},{9,7},{10,... | collective-permute-start | bytes 6291464 | tf_op jit(solution)/shard_map/ppermute | solution.py:30
  6.4 1.6 copy-done
  8.0 1.4 shard_map.17
  9.5 41.6 %collective-permute-done.refs_1_ = f32[512,1024]{1,0:T(8,128)S(1)} collective-permute-done((f32[512,1024]{1,0:T(8,128)}, f32[512,1024]{1,0:T(8,128)S(1)}, u32[]{:S(2)}, u32[]{:S(2)}) %collective-permute-start) | collective-permute-done | bytes 2097184 | tf_op jit(solution)/shard_map/ppermute | solution.py:30
  51.1 3.4 %collective-permute-done.1.refs_0_ = f32[512,1024]{1,0:T(8,128)} collective-permute-done((f32[512,1024]{1,0:T(8,128)}, f32[512,1024]{1,0:T(8,128)}, u32[]{:S(2)}, u32[]{:S(2)}) %collective-permute-start.1) | collective-permute-done | bytes 2097184 | tf_op jit(solution)/shard_map/ppermute | solution.py:30
  54.8 3.0 %collective-permute-start.3 = (f32[192,1024]{1,0:T(8,128)S(1)}, f32[192,1024]{1,0:T(8,128)S(1)}, u32[]{:S(2)}, u32[]{:S(2)}) collective-permute-start(f32[192,1024]{1,0:T(8,128)S(1)} %slice.24), channel_id=1, source_target_pairs={{0,14},{1,15},{2,0},{3,1},{4,2},{5,3},{6,4},{7,5},{8,6},{9,7},{10,... | collective-permute-start | bytes 2359304 | tf_op jit(solution)/shard_map/ppermute | solution.py:30
  57.9 1.2 slice.25
  59.2 1.4 slice.27
  60.6 3.4 %shard_map.18 = (bf16[512,1024]{1,0:T(8,128)(2,1)S(1)}, bf16[512,1024]{1,0:T(8,128)(2,1)S(1)}, bf16[512,1024]{1,0:T(8,128)(2,1)S(1)}, bf16[512,1024]{1,0:T(8,128...) custom-call(s32[4]{0:T(128)S(1)} %pad_add_fusion.place_ref, ...), custom_call_target="tpu_custom_call" | custom-call | tf_op jit(solution)/shard_map/pallas_call | solution.py:54
  64.1 8.7 %shard_map.19 = (f32[256,2048]{1,0:T(8,128)S(1)}, f32[256,2048]{1,0:T(8,128)S(1)}) custom-call(s32[4]{0:T(128)S(1)} %pad_add_fusion.place_ref, bf16[512,1024]{1,0:T(8,128)(2,1)S(1)} %get-tuple-element.81.refs_0_.refs_4_, bf16[512,1024]{1,0:T(8,128)(2,1)S(1)} %get-tuple-element.82.refs_1_.refs_5_, bf16[512,1024]{1,0:T(8,128)(2,1)S(1)} %get-tuple-element.83.refs_2_, ...), custom_call_target="tpu_custom_call" | custom-call | tf_op jit(solution)/shard_map/pallas_call | solution.py:54
  73.2 4.7 %collective-permute-done.4.refs_0_ = f32[192,1024]{1,0:T(8,128)S(1)} collective-permute-done((f32[192,1024]{1,0:T(8,128)S(1)}, f32[192,1024]{1,0:T(8,128)S(1)}, u32[]{:S(2)}, u32[]{:S(2)}) %collective-permute-start.4) | collective-permute-done | bytes 786464 | tf_op jit(solution)/shard_map/ppermute | solution.py:30
  77.9 2.0 %collective-permute-start.6 = (f32[320,1024]{1,0:T(8,128)S(1)}, f32[320,1024]{1,0:T(8,128)S(1)}, u32[]{:S(2)}, u32[]{:S(2)}) collective-permute-start(f32[320,1024]{1,0:T(8,128)S(1)} %slice.27), channel_id=1, source_target_pairs={{0,2},{1,3},{2,4},{3,5},{4,6},{5,7},{6,8},{7,9},{8,10},{9,11},{10,... | collective-permute-start | bytes 3932168 | tf_op jit(solution)/shard_map/ppermute | solution.py:30
  80.4 1.6 collective-permute-done.8.got
  82.8 18.0 %collective-permute-done.7.refs_0_ = f32[192,1024]{1,0:T(8,128)S(1)} collective-permute-done((f32[192,1024]{1,0:T(8,128)S(1)}, f32[192,1024]{1,0:T(8,128)S(1)}, u32[]{:S(2)}, u32[]{:S(2)}) %collective-permute-start.7) | collective-permute-done | bytes 786464 | tf_op jit(solution)/shard_map/ppermute | solution.py:30
  100.8 8.3 %collective-permute-done.5.refs_3_ = f32[320,1024]{1,0:T(8,128)S(1)} collective-permute-done((f32[320,1024]{1,0:T(8,128)S(1)}, f32[320,1024]{1,0:T(8,128)S(1)}, u32[]{:S(2)}, u32[]{:S(2)}) %collective-permute-start.5) | collective-permute-done | bytes 1310752 | tf_op jit(solution)/shard_map/ppermute | solution.py:30
  109.0 1.2 collective-permute-done.6.refs_1_
  110.8 1.6 collective-permute-start.10
  112.3 1.7 collective-permute-start.11
  114.0 2.0 collective-permute-start.12
  116.0 1.4 shard_map.21
  117.4 6.7 %shard_map.22 = (f32[256,1536]{1,0:T(8,128)S(1)}, f32[256,1536]{1,0:T(8,128)S(1)}) custom-call(s32[4]{0:T(128)S(1)} %pad_add_fusion.place_ref, bf16[512,1024]{1,0:T(8,128)(2,1)S(1)} %get-tuple-element.104.refs_0_.refs_8_, bf16[512,1024]{1,0:T(8,128)(2,1)S(1)} %get-tuple-element.105.refs_1_.refs_9_, bf16[512,1024]{1,0:T(8,128)(2,1)S(1)} %get-tuple-element.85.refs_4_.refs_2_, ...), custom_call_target="tpu_custom_call" | custom-call | tf_op jit(solution)/shard_map/pallas_call | solution.py:54
  124.1 1.6 collective-permute-done.10.a
  125.7 1.5 collective-permute-done.11.b
  127.2 10.5 %collective-permute-done.12.d = f32[64,2048]{1,0:T(8,128)S(1)} collective-permute-done((f32[64,2048]{1,0:T(8,128)S(1)}, f32[64,2048]{1,0:T(8,128)S(1)}, u32[]{:S(2)}, u32[]{:S(2)}) %collective-permute-start.12) | collective-permute-done | bytes 524320 | tf_op jit(solution)/shard_map/ppermute | solution.py:30
  138.4 3.8 %collective-permute-done.9.refs_1_ = f32[320,1024]{1,0:T(8,128)S(1)} collective-permute-done((f32[320,1024]{1,0:T(8,128)S(1)}, f32[320,1024]{1,0:T(8,128)S(1)}, u32[]{:S(2)}, u32[]{:S(2)}) %collective-permute-start.9) | collective-permute-done | bytes 1310752 | tf_op jit(solution)/shard_map/ppermute | solution.py:30
  142.2 0.9 shard_map.23
  143.0 4.8 %shard_map.24 = (f32[256,2560]{1,0:T(8,128)S(1)}, f32[256,2560]{1,0:T(8,128)S(1)}) custom-call(s32[4]{0:T(128)S(1)} %pad_add_fusion.place_ref, bf16[512,1024]{1,0:T(8,128)(2,1)S(1)} %get-tuple-element.79.refs_6_.refs_0_, bf16[512,1024]{1,0:T(8,128)(2,1)S(1)} %get-tuple-element.80.refs_7_.refs_1_, bf16[512,1024]{1,0:T(8,128)(2,1)S(1)} %get-tuple-element.111.refs_2_, ...), custom_call_target="tpu_custom_call" | custom-call | tf_op jit(solution)/shard_map/pallas_call | solution.py:54
  148.0 4.9 %collective-permute-done.14.got = f32[256,2560]{1,0:T(8,128)S(1)} collective-permute-done((f32[256,2560]{1,0:T(8,128)S(1)}, f32[256,2560]{1,0:T(8,128)S(1)}, u32[]{:S(2)}, u32[]{:S(2)}) %collective-permute-start.14) | collective-permute-done | bytes 2621472 | tf_op jit(solution)/shard_map/ppermute | solution.py:30
  152.9 0.8 shard_map.26
  153.7 1.3 collective-permute-start.18
  155.0 1.6 collective-permute-start.15
  156.5 1.7 collective-permute-start.16
  158.2 2.0 collective-permute-start.17
  160.2 0.8 collective-permute-start.13
  161.0 6.1 %collective-permute-done.15.a = f32[64,1536]{1,0:T(8,128)S(1)} collective-permute-done((f32[64,1536]{1,0:T(8,128)S(1)}, f32[64,1536]{1,0:T(8,128)S(1)}, u32[]{:S(2)}, u32[]{:S(2)}) %collective-permute-start.15) | collective-permute-done | bytes 393248 | tf_op jit(solution)/shard_map/ppermute | solution.py:30
  167.1 1.5 collective-permute-done.16.b
  168.6 8.1 %collective-permute-done.17.d = f32[64,1536]{1,0:T(8,128)S(1)} collective-permute-done((f32[64,1536]{1,0:T(8,128)S(1)}, f32[64,1536]{1,0:T(8,128)S(1)}, u32[]{:S(2)}, u32[]{:S(2)}) %collective-permute-start.17) | collective-permute-done | bytes 393248 | tf_op jit(solution)/shard_map/ppermute | solution.py:30
  177.4 1.2 collective-permute-start.19
  178.6 2.1 %collective-permute-start.20 = (f32[32,1024]{1,0:T(8,128)S(1)}, f32[32,1024]{1,0:T(8,128)S(1)}, u32[]{:S(2)}, u32[]{:S(2)}) collective-permute-start(f32[32,1024]{1,0:T(8,128)S(1)} %get-tuple-element.135), channel_id=1, source_target_pairs={{0,192},{1,193},{2,194},{3,195},{4,196},{5,197},{6,198},{7,199},{8... | collective-permute-start | bytes 393224 | tf_op jit(solution)/shard_map/ppermute | solution.py:30
  181.4 0.8 collective-permute-start.24
  182.2 1.9 collective-permute-done.19
  184.1 1.1 collective-permute-done.20
  185.2 2.0 collective-permute-done.21
  187.3 1.1 collective-permute-start.26
  188.5 1.8 collective-permute-start.25
  190.3 4.3 %collective-permute-done.22 = f32[32,512]{1,0:T(8,128)S(1)} collective-permute-done((f32[32,512]{1,0:T(8,128)S(1)}, f32[32,512]{1,0:T(8,128)S(1)}, u32[]{:S(2)}, u32[]{:S(2)}) %collective-permute-start.22) | collective-permute-done | bytes 65568 | tf_op jit(solution)/shard_map/ppermute | solution.py:30
  194.6 6.2 %collective-permute-done.25 = f32[32,1536]{1,0:T(8,128)S(1)} collective-permute-done((f32[32,1536]{1,0:T(8,128)S(1)}, f32[32,1536]{1,0:T(8,128)S(1)}, u32[]{:S(2)}, u32[]{:S(2)}) %collective-permute-start.25) | collective-permute-done | bytes 196640 | tf_op jit(solution)/shard_map/ppermute | solution.py:30
  200.9 0.8 copy-done.1
  (40 shorter events, 5.6 us)
Async XLA Ops:
  0.0 51.1 %collective-permute-start = (f32[512,1024]{1,0:T(8,128)}, f32[512,1024]{1,0:T(8,128)S(1)}, u32[]{:S(2)}, u32[]{:S(2)}) collective-permute-start(f32[512,1024]{1,0:T(8,128)} %bitcast.34), channel_id=1, source_target_pairs={{0,14},{1,15},{2,0},{3,1},{4,2},{5,3},{6,4},{7,5},{8,6},{9,7},{10,... | collective-permute-start | bytes 6291464 | tf_op jit(solution)/shard_map/ppermute | solution.py:30
  5.9 48.6 %collective-permute-start.1 = (f32[512,1024]{1,0:T(8,128)}, f32[512,1024]{1,0:T(8,128)}, u32[]{:S(2)}, u32[]{:S(2)}) collective-permute-start(f32[512,1024]{1,0:T(8,128)} %bitcast.35), channel_id=1, source_target_pairs={{0,2},{1,3},{2,4},{3,5},{4,6},{5,7},{6,8},{7,9},{8,10},{9,11},{10,... | collective-permute-start | bytes 6291464 | tf_op jit(solution)/shard_map/ppermute | solution.py:30
  5.9 48.9 %collective-permute-start.2 = (f32[512,1024]{1,0:T(8,128)}, f32[512,1024]{1,0:T(8,128)}, u32[]{:S(2)}, u32[]{:S(2)}) collective-permute-start(f32[512,1024]{1,0:T(8,128)} %bitcast.36), channel_id=1, source_target_pairs={{0,1},{1,0},{2,3},{3,2},{4,5},{5,4},{6,7},{7,6},{8,9},{9,8},{10,11... | collective-permute-start | bytes 6291464 | tf_op jit(solution)/shard_map/ppermute | solution.py:30
  6.4 1.6 copy-start
  54.8 18.3 %collective-permute-start.3 = (f32[192,1024]{1,0:T(8,128)S(1)}, f32[192,1024]{1,0:T(8,128)S(1)}, u32[]{:S(2)}, u32[]{:S(2)}) collective-permute-start(f32[192,1024]{1,0:T(8,128)S(1)} %slice.24), channel_id=1, source_target_pairs={{0,14},{1,15},{2,0},{3,1},{4,2},{5,3},{6,4},{7,5},{8,6},{9,7},{10,... | collective-permute-start | bytes 2359304 | tf_op jit(solution)/shard_map/ppermute | solution.py:30
  59.0 18.8 %collective-permute-start.4 = (f32[192,1024]{1,0:T(8,128)S(1)}, f32[192,1024]{1,0:T(8,128)S(1)}, u32[]{:S(2)}, u32[]{:S(2)}) collective-permute-start(f32[192,1024]{1,0:T(8,128)S(1)} %slice.25), channel_id=1, source_target_pairs={{0,2},{1,3},{2,4},{3,5},{4,6},{5,7},{6,8},{7,9},{8,10},{9,11},{10,... | collective-permute-start | bytes 2359304 | tf_op jit(solution)/shard_map/ppermute | solution.py:30
  77.8 4.2 %collective-permute-start.8 = (f32[256,2048]{1,0:T(8,128)S(1)}, f32[256,2048]{1,0:T(8,128)S(1)}, u32[]{:S(2)}, u32[]{:S(2)}) collective-permute-start(f32[256,2048]{1,0:T(8,128)S(1)} %get-tuple-element.95), channel_id=1, source_target_pairs={{0,16},{1,17},{2,18},{3,19},{4,20},{5,21},{6,22},{7,23},{8,24},{9,... | collective-permute-start | bytes 6291464 | tf_op jit(solution)/shard_map/ppermute | solution.py:30
  77.9 31.2 %collective-permute-start.5 = (f32[320,1024]{1,0:T(8,128)S(1)}, f32[320,1024]{1,0:T(8,128)S(1)}, u32[]{:S(2)}, u32[]{:S(2)}) collective-permute-start(f32[320,1024]{1,0:T(8,128)S(1)} %slice.26), channel_id=1, source_target_pairs={{0,14},{1,15},{2,0},{3,1},{4,2},{5,3},{6,4},{7,5},{8,6},{9,7},{10,... | collective-permute-start | bytes 3932168 | tf_op jit(solution)/shard_map/ppermute | solution.py:30
  77.9 32.4 %collective-permute-start.6 = (f32[320,1024]{1,0:T(8,128)S(1)}, f32[320,1024]{1,0:T(8,128)S(1)}, u32[]{:S(2)}, u32[]{:S(2)}) collective-permute-start(f32[320,1024]{1,0:T(8,128)S(1)} %slice.27), channel_id=1, source_target_pairs={{0,2},{1,3},{2,4},{3,5},{4,6},{5,7},{6,8},{7,9},{8,10},{9,11},{10,... | collective-permute-start | bytes 3932168 | tf_op jit(solution)/shard_map/ppermute | solution.py:30
  79.9 20.9 %collective-permute-start.7 = (f32[192,1024]{1,0:T(8,128)S(1)}, f32[192,1024]{1,0:T(8,128)S(1)}, u32[]{:S(2)}, u32[]{:S(2)}) collective-permute-start(f32[192,1024]{1,0:T(8,128)S(1)} %collective-permute-done.3.refs_2_), channel_id=1, source_target_pairs={{0,1},{1,0},{2,3},{3,2},{4,5},{5,4},{6,7},{7,6},{8,9},{9,8},{10,11... | collective-permute-start | bytes 2359304 | tf_op jit(solution)/shard_map/ppermute | solution.py:30
  110.3 31.9 %collective-permute-start.9 = (f32[320,1024]{1,0:T(8,128)S(1)}, f32[320,1024]{1,0:T(8,128)S(1)}, u32[]{:S(2)}, u32[]{:S(2)}) collective-permute-start(f32[320,1024]{1,0:T(8,128)S(1)} %collective-permute-done.5.refs_3_), channel_id=1, source_target_pairs={{0,1},{1,0},{2,3},{3,2},{4,5},{5,4},{6,7},{7,6},{8,9},{9,8},{10,11... | collective-permute-start | bytes 3932168 | tf_op jit(solution)/shard_map/ppermute | solution.py:30
  110.8 14.9 %collective-permute-start.10 = (f32[64,2048]{1,0:T(8,128)S(1)}, f32[64,2048]{1,0:T(8,128)S(1)}, u32[]{:S(2)}, u32[]{:S(2)}) collective-permute-start(f32[64,2048]{1,0:T(8,128)S(1)} %get-tuple-element.118), channel_id=1, source_target_pairs={{0,64},{1,65},{2,66},{3,67},{4,68},{5,69},{6,70},{7,71},{8,72},{9,... | collective-permute-start | bytes 1572872 | tf_op jit(solution)/shard_map/ppermute | solution.py:30
  112.3 14.9 %collective-permute-start.11 = (f32[64,2048]{1,0:T(8,128)S(1)}, f32[64,2048]{1,0:T(8,128)S(1)}, u32[]{:S(2)}, u32[]{:S(2)}) collective-permute-start(f32[64,2048]{1,0:T(8,128)S(1)} %get-tuple-element.119), channel_id=1, source_target_pairs={{0,192},{1,193},{2,194},{3,195},{4,196},{5,197},{6,198},{7,199},{8... | collective-permute-start | bytes 1572872 | tf_op jit(solution)/shard_map/ppermute | solution.py:30
  114.0 23.7 %collective-permute-start.12 = (f32[64,2048]{1,0:T(8,128)S(1)}, f32[64,2048]{1,0:T(8,128)S(1)}, u32[]{:S(2)}, u32[]{:S(2)}) collective-permute-start(f32[64,2048]{1,0:T(8,128)S(1)} %get-tuple-element.120), channel_id=1, source_target_pairs={{0,128},{1,129},{2,130},{3,131},{4,132},{5,133},{6,134},{7,135},{8... | collective-permute-start | bytes 1572872 | tf_op jit(solution)/shard_map/ppermute | solution.py:30
  147.9 5.0 %collective-permute-start.14 = (f32[256,2560]{1,0:T(8,128)S(1)}, f32[256,2560]{1,0:T(8,128)S(1)}, u32[]{:S(2)}, u32[]{:S(2)}) collective-permute-start(f32[256,2560]{1,0:T(8,128)S(1)} %get-tuple-element.126), channel_id=1, source_target_pairs={{0,16},{1,17},{2,18},{3,19},{4,20},{5,21},{6,22},{7,23},{8,24},{9,... | collective-permute-start | bytes 7864328 | tf_op jit(solution)/shard_map/ppermute | solution.py:30
  153.7 23.0 %collective-permute-start.18 = (f32[128,1024]{1,0:T(8,128)S(1)}, f32[128,1024]{1,0:T(8,128)S(1)}, u32[]{:S(2)}, u32[]{:S(2)}) collective-permute-start(f32[128,1024]{1,0:T(8,128)S(1)} %get-tuple-element.132), channel_id=1, source_target_pairs={{0,32},{1,33},{2,34},{3,35},{4,36},{5,37},{6,38},{7,39},{8,40},{9,... | collective-permute-start | bytes 1572872 | tf_op jit(solution)/shard_map/ppermute | solution.py:30
  155.0 12.1 %collective-permute-start.15 = (f32[64,1536]{1,0:T(8,128)S(1)}, f32[64,1536]{1,0:T(8,128)S(1)}, u32[]{:S(2)}, u32[]{:S(2)}) collective-permute-start(f32[64,1536]{1,0:T(8,128)S(1)} %get-tuple-element.128), channel_id=1, source_target_pairs={{0,64},{1,65},{2,66},{3,67},{4,68},{5,69},{6,70},{7,71},{8,72},{9,... | collective-permute-start | bytes 1179656 | tf_op jit(solution)/shard_map/ppermute | solution.py:30
  156.5 12.0 %collective-permute-start.16 = (f32[64,1536]{1,0:T(8,128)S(1)}, f32[64,1536]{1,0:T(8,128)S(1)}, u32[]{:S(2)}, u32[]{:S(2)}) collective-permute-start(f32[64,1536]{1,0:T(8,128)S(1)} %get-tuple-element.129), channel_id=1, source_target_pairs={{0,192},{1,193},{2,194},{3,195},{4,196},{5,197},{6,198},{7,199},{8... | collective-permute-start | bytes 1179656 | tf_op jit(solution)/shard_map/ppermute | solution.py:30
  158.2 18.5 %collective-permute-start.17 = (f32[64,1536]{1,0:T(8,128)S(1)}, f32[64,1536]{1,0:T(8,128)S(1)}, u32[]{:S(2)}, u32[]{:S(2)}) collective-permute-start(f32[64,1536]{1,0:T(8,128)S(1)} %get-tuple-element.130), channel_id=1, source_target_pairs={{0,128},{1,129},{2,130},{3,131},{4,132},{5,133},{6,134},{7,135},{8... | collective-permute-start | bytes 1179656 | tf_op jit(solution)/shard_map/ppermute | solution.py:30
  160.2 20.6 %collective-permute-start.13 = (f32[32,2048]{1,0:T(8,128)S(1)}, f32[32,2048]{1,0:T(8,128)S(1)}, u32[]{:S(2)}, u32[]{:S(2)}) collective-permute-start(f32[32,2048]{1,0:T(8,128)S(1)} %get-tuple-element.124), channel_id=1, source_target_pairs={{0,32},{1,33},{2,34},{3,35},{4,36},{5,37},{6,38},{7,39},{8,40},{9,... | collective-permute-start | bytes 786440 | tf_op jit(solution)/shard_map/ppermute | solution.py:30
  177.4 6.7 %collective-permute-start.19 = (f32[32,1024]{1,0:T(8,128)S(1)}, f32[32,1024]{1,0:T(8,128)S(1)}, u32[]{:S(2)}, u32[]{:S(2)}) collective-permute-start(f32[32,1024]{1,0:T(8,128)S(1)} %get-tuple-element.134), channel_id=1, source_target_pairs={{0,64},{1,65},{2,66},{3,67},{4,68},{5,69},{6,70},{7,71},{8,72},{9,... | collective-permute-start | bytes 393224 | tf_op jit(solution)/shard_map/ppermute | solution.py:30
  178.6 6.6 %collective-permute-start.20 = (f32[32,1024]{1,0:T(8,128)S(1)}, f32[32,1024]{1,0:T(8,128)S(1)}, u32[]{:S(2)}, u32[]{:S(2)}) collective-permute-start(f32[32,1024]{1,0:T(8,128)S(1)} %get-tuple-element.135), channel_id=1, source_target_pairs={{0,192},{1,193},{2,194},{3,195},{4,196},{5,197},{6,198},{7,199},{8... | collective-permute-start | bytes 393224 | tf_op jit(solution)/shard_map/ppermute | solution.py:30
  180.7 6.5 %collective-permute-start.21 = (f32[32,1024]{1,0:T(8,128)S(1)}, f32[32,1024]{1,0:T(8,128)S(1)}, u32[]{:S(2)}, u32[]{:S(2)}) collective-permute-start(f32[32,1024]{1,0:T(8,128)S(1)} %get-tuple-element.136), channel_id=1, source_target_pairs={{0,128},{1,129},{2,130},{3,131},{4,132},{5,133},{6,134},{7,135},{8... | collective-permute-start | bytes 393224 | tf_op jit(solution)/shard_map/ppermute | solution.py:30
  180.8 9.4 %collective-permute-start.23 = (f32[32,1024]{1,0:T(8,128)S(1)}, f32[32,1024]{1,0:T(8,128)S(1)}, u32[]{:S(2)}, u32[]{:S(2)}) collective-permute-start(f32[32,1024]{1,0:T(8,128)S(1)} %slice.32), channel_id=1, source_target_pairs={{0,14},{1,15},{2,0},{3,1},{4,2},{5,3},{6,4},{7,5},{8,6},{9,7},{10,... | collective-permute-start | bytes 393224 | tf_op jit(solution)/shard_map/ppermute | solution.py:30
  181.4 7.0 %collective-permute-start.24 = (f32[32,1536]{1,0:T(8,128)S(1)}, f32[32,1536]{1,0:T(8,128)S(1)}, u32[]{:S(2)}, u32[]{:S(2)}) collective-permute-start(f32[32,1536]{1,0:T(8,128)S(1)} %get-tuple-element.138), channel_id=1, source_target_pairs={{0,32},{1,33},{2,34},{3,35},{4,36},{5,37},{6,38},{7,39},{8,40},{9,... | collective-permute-start | bytes 589832 | tf_op jit(solution)/shard_map/ppermute | solution.py:30
  187.2 7.4 %collective-permute-start.22 = (f32[32,512]{1,0:T(8,128)S(1)}, f32[32,512]{1,0:T(8,128)S(1)}, u32[]{:S(2)}, u32[]{:S(2)}) collective-permute-start(f32[32,512]{1,0:T(8,128)S(1)} %get-tuple-element.140), channel_id=1, source_target_pairs={{0,12},{1,13},{2,14},{3,15},{4,0},{5,1},{6,2},{7,3},{8,4},{9,5},{1... | collective-permute-start | bytes 196616 | tf_op jit(solution)/shard_map/ppermute | solution.py:30
  187.3 13.5 %collective-permute-start.26 = (f32[32,512]{1,0:T(8,128)S(1)}, f32[32,512]{1,0:T(8,128)S(1)}, u32[]{:S(2)}, u32[]{:S(2)}) collective-permute-start(f32[32,512]{1,0:T(8,128)S(1)} %get-tuple-element.139), channel_id=1, source_target_pairs={{0,14},{1,15},{2,0},{3,1},{4,2},{5,3},{6,4},{7,5},{8,6},{9,7},{10,... | collective-permute-start | bytes 196616 | tf_op jit(solution)/shard_map/ppermute | solution.py:30
  188.5 12.3 %collective-permute-start.25 = (f32[32,1536]{1,0:T(8,128)S(1)}, f32[32,1536]{1,0:T(8,128)S(1)}, u32[]{:S(2)}, u32[]{:S(2)}) collective-permute-start(f32[32,1536]{1,0:T(8,128)S(1)} %add.35), channel_id=1, source_target_pairs={{0,12},{1,13},{2,14},{3,15},{4,0},{5,1},{6,2},{7,3},{8,4},{9,5},{1... | collective-permute-start | bytes 589832 | tf_op jit(solution)/shard_map/ppermute | solution.py:30
  200.9 0.8 copy-start.1

commit v3 on v2

--- a/solution.py
+++ b/solution.py
@@ -10,7 +10,7 @@
 NY, NXL, NC, NZ, NXH = 4, 2, 2, 8, 2
 TILE = 512
 SHARE = 32
-HEAD = 192
+HALF = 256
 
 
 def place(y, xl, c, z, xh):
@@ -114,7 +114,7 @@
     rows, columns = [number(pair) for pair in rows], [number(pair) for pair in columns]
     outs = call(
         functools.partial(split_kernel, rows, columns, len(arrays)),
-        [(TILE, depth)] * (2 * len(rows + columns)),
+        [(sum(arrays[at].shape[0] for at, _ in pair[0]), depth) for pair in rows + columns for _ in range(2)],
         [place_now, *arrays],
         24,
         jnp.bfloat16,
@@ -131,25 +131,27 @@
     def dot(a, b):
         return lax.dot_general(a, b, (((1,), (1,)), ((), ())), preferred_element_type=jnp.float32)
 
-    def write(t, tile):
+    def write(at, tile):
         rh, rl, ch, cl = tile
 
-        @pl.loop(0, 2)
+        @pl.loop(0, operands[ch].shape[0] // HALF)
         def _(half):
-            part = pl.ds(pl.multiple_of(half * 256, 256), 256)
+            part = pl.ds(pl.multiple_of(half * HALF, HALF), HALF)
             ah, al = operands[rh][...], operands[rl][...]
             bh, bl = operands[ch][part, :], operands[cl][part, :]
             v = dot(ah, bh) + dot(ah, bl) + dot(al, bh)
-            to = pl.ds(pl.multiple_of(before + t * TILE + half * 256, 256), 256)
+            to = pl.ds(pl.multiple_of(at + half * HALF, HALF), HALF)
             mine[:, to] = v[:256]
             other[:, to] = v[256:]
 
-    for t, tile in enumerate(tiles):
-        write(t, tile)
+    at = before
+    for tile in tiles:
+        write(at, tile)
+        at += operands[tile[2]].shape[0]
     for column_of_chips, tile in enumerate(either):
         @pl.when(place_ref[3] == column_of_chips)
         def _():
-            write(len(tiles), tile)
+            write(at, tile)
 
 
 def products(place_now, pairs, before=(), either=()):
@@ -165,7 +167,7 @@
     number = lambda some: [tuple(index_of(array) for array in rows + columns) for rows, columns in some]
     tiles, either = number(pairs), number(either)
     start = before[0].shape[1] if before else 0
-    width = start + TILE * (len(tiles) + bool(either))
+    width = start + sum(arrays[tile[2]].shape[0] for tile in tiles + either[:1])
     kernel = functools.partial(products_kernel, tiles, either, len(arrays), start)
     return call(kernel, [(256, width)] * 2, [place_now, *arrays, *before], 28)
 
@@ -186,14 +188,17 @@
     return call(cores_kernel, [(64, mine.shape[1])] * NY, [place_now, mine, send(other, swap_core)], 10)
 
 
-def mixed_cores_kernel(width, place_ref, mine, got, *outs):
+def mixed_cores_kernel(by_y_halves, by_x_halves, place_ref, mine, got, *outs):
     by_y, by_x = outs[:NY], outs[NY:]
     for r in range(NY):
-        rows = pl.ds(r * 64, 64)
-        by_y[r][...] = mine[rows, :width] + got[rows, :width]
-        for x in range(NXL):
-            rows = pl.ds(r * 64 + x * SHARE, SHARE)
-            by_x[x][pl.ds(r * SHARE, SHARE), :] = mine[rows, width:] + got[rows, width:]
+        for i, h in enumerate(by_y_halves):
+            rows, from_, to = pl.ds(r * 64, 64), pl.ds(h * HALF, HALF), pl.ds(i * HALF, HALF)
+            by_y[r][:, to] = mine[rows, from_] + got[rows, from_]
+        for i, h in enumerate(by_x_halves):
+            from_, to = pl.ds(h * HALF, HALF), pl.ds(i * HALF, HALF)
+            for x in range(NXL):
+                rows = pl.ds(r * 64 + x * SHARE, SHARE)
+                by_x[x][pl.ds(r * SHARE, SHARE), to] = mine[rows, from_] + got[rows, from_]
 
 
 def mixed_kernel(place_ref, kept, a, b, d, kept_x, got_x, mine, other, *outs):
@@ -203,21 +208,18 @@
         outs[r][...] = kept_x[rows, :] + got_x[rows, :]
 
 
-def mixed_sum(place_now, mine, other, width):
-    rest = mine.shape[1] - width
-    shapes = [(64, width)] * NY + [(NY * SHARE, rest)] * NXL
-    outs = call(functools.partial(mixed_cores_kernel, width), shapes, [place_now, mine, send(other, swap_core)], 12)
+def mixed_sum(place_now, mine, other, by_y_halves, by_x_halves):
+    wide, rest = HALF * len(by_y_halves), HALF * len(by_x_halves)
+    kernel = functools.partial(mixed_cores_kernel, by_y_halves, by_x_halves)
+    shapes = [(64, wide)] * NY + [(NY * SHARE, rest)] * NXL
+    outs = call(kernel, shapes, [place_now, mine, send(other, swap_core)], 12)
     by_y, by_x = outs[:NY], outs[NY:]
     got = [send(by_y[r], y_by(r)) for r in (1, 3, 2)] + [by_x[0], send(by_x[1], swap_xl)]
-    shapes = [(SHARE, width)] * 2 + [(SHARE, rest)] * NY
+    shapes = [(SHARE, wide)] * 2 + [(SHARE, rest)] * NY
     mine, other, *by_y = call(mixed_kernel, shapes, [place_now, by_y[0], *got], 8)
+    first = mine + send(other, swap_xl)
     got = [send(by_y[r], y_by(r)) for r in (1, 3, 2)]
-    return mine + send(other, swap_xl), by_y[0] + got[0] + got[1] + got[2]
-
-
-def over_y(place_now, parts):
-    got = [send(parts[r], y_by(r)) for r in (1, 3, 2)]
-    return call(ys_kernel, [(SHARE, parts[0].shape[1])] * 2, [place_now, parts[0], *got], 4)
+    return first, by_y[0] + got[0] + got[1] + got[2]
 
 
 def over_x(mine, other):
@@ -236,7 +238,7 @@
     p1, m1, o0 = send(own, z_by(-1)), send(own, z_by(1)), send(own, swap_xh)
     p1, m1, o0, rows_own, cols_own = tie((p1, m1, o0, rows_own, cols_own))
 
-    p1a, p1b, m1a, m1b = p1[:HEAD], p1[HEAD:], m1[:HEAD], m1[HEAD:]
+    p1a, p1b, m1a, m1b = p1[:HALF], p1[HALF:], m1[:HALF], m1[HALF:]
     p2a, m2a = send(p1a, z_by(-1)), send(m1a, z_by(1))
     rows_m1, cols_p1, cols_o0 = split(place_now, [whole(m1)], [whole(p1), whole(o0)])
     product1 = products(
@@ -249,20 +251,28 @@
     p2b, m2b, o2a, parts1 = tie((p2b, m2b, o2a, parts1))
 
     o2b = send(p2b, swap_xh)
-    sums1 = over_y(place_now, parts1)
-    rows_m2, cols_p2 = split(place_now, [whole(m2a, m2b)], [whole(p2a, p2b)])
-    product2 = products(place_now, [(rows_m2, cols) for cols in (cols_p1, cols_p2, cols_o0)])
+    got1 = [send(parts1[r], y_by(r)) for r in (1, 3, 2)]
+    rows_m2, cols_p2, cols_o2a = split(place_now, [whole(m2a, m2b)], [whole(p2a, p2b), whole(o2a)])
+    cols_o0a, cols_o0b = [[v[start:start + HALF] for v in cols_o0] for start in (0, HALF)]
+    product2 = products(
+        place_now,
+        [(rows_m2, cols_p2), (rows_m2, cols_o0), (rows_m1, cols_p2), (rows_m1, cols_o2a)],
+        (),
+        ((rows_own, tuple(cols_o0a)), (rows_m2, cols_o2a)),
+    )
     o2b, product2 = tie((o2b, product2))
-    o2 = ((o2a, 0), (o2b, 0))
-    (cols_o2,) = split(place_now, [], [(o2, o2)])
-    product2 = products(place_now, [(rows_m1, cols_o2)], product2, ((rows_own, cols_o0), (rows_m2, cols_o2)))
-    product2, sums1 = tie((product2, sums1))
-    far, v = mixed_sum(place_now, *product2, 1536)
-    d3, d4, t2 = jnp.split(send(far, z_by(-2)), 3, 1)
-    t3, x = send(v[:, :512], z_by(-1)), v[:, 512:]
-    x = jnp.where(first, x, send(x, z_by(-2)))
-
-    v = over_x(*sums1)
+    (cols_o2b,) = split(place_now, [], [whole(o2b)])
+    product2 = products(
+        place_now, [(rows_m1, cols_o2b)], product2, ((rows_own, tuple(cols_o0b)), (rows_m2, cols_o2b))
+    )
+    product2, parts1, got1 = tie((product2, parts1, got1))
+    far, v = mixed_sum(place_now, *product2, (0, 1, 2, 3, 7, 9), (4, 5, 6, 8))
+    x = far[:, 1024:]
+    d4, t2, far = jnp.split(send(far, z_by(-2)), 3, 1)
+    d3, t3 = jnp.split(send(v, z_by(-1)), 2, 1)
+    x = jnp.where(first, x, far)
+
+    v = over_x(*call(ys_kernel, [(SHARE, parts1[0].shape[1])] * 2, [place_now, parts1[0], *got1], 4))
     d0, d1 = jnp.split(v[:, :1024], 2, 1)
     d2, t1 = jnp.split(send(v[:, 1024:], z_by(-1)), 2, 1)
 

time: 202 us -> 196 us (0.970)
  waiting for transfers between devices: 133 us -> 123 us
    ppermute x27 -> x26, waiting for transfers between devices: 133 us -> 123 us  [send(): return lax.ppermute(value, ('aux', 'bas'), pairs)]
    ppermute x27 -> x26, starting transfers between devices: 32.9 us -> 34.1 us  [send(): return lax.ppermute(value, ('aux', 'bas'), pairs)]
  transfers between devices with their start and end apart: 27 -> 26, of which waited for: 22 -> 16; matrix products, arithmetic and copies ran while one was open for 1% -> 2% of each run, Pallas kernels for 12% -> 15%
where the time goes in v3:
time: 196 us; the launch traced here: 195 us
  waiting for transfers between devices  123 us (63%)
  starting transfers between devices  34.1 us (17%)
  Pallas kernels  31.8 us (16%)
  local copies, waits for them, and re-layouts  4.53 us (2%)
    ppermute x26, waiting for transfers between devices, send(): return lax.ppermute(value, ('aux', 'bas'), pairs)  123 us
    ppermute x26, starting transfers between devices, send(): return lax.ppermute(value, ('aux', 'bas'), pairs)  34.1 us
    pallas_call x11, Pallas kernels, call(): pl.pallas_call(kernel, out_shape=[jax.ShapeDtypeStruct(shape, dtype) for...  31.8 us
  transfers between devices with their start and end apart: 26, of which 16 were waited for; matrix products, arithmetic and copies ran while one was open for 2% of the time, Pallas kernels for 15%

profile of v3, /device:TPU:4, one launch (start us, length us, event | category | flops | bytes accessed | tf_op | source)
XLA Modules:
  0.0 195.1 jit_solution(14341868754738083791)
XLA Ops:
  0.0 5.9 %collective-permute-start = (f32[512,1024]{1,0:T(8,128)}, f32[512,1024]{1,0:T(8,128)S(1)}, u32[]{:S(2)}, u32[]{:S(2)}) collective-permute-start(f32[512,1024]{1,0:T(8,128)} %bitcast.34), channel_id=1, source_target_pairs={{0,14},{1,15},{2,0},{3,1},{4,2},{5,3},{6,4},{7,5},{8,6},{9,7},{10,... | collective-permute-start | bytes 6291464 | tf_op jit(solution)/shard_map/ppermute | solution.py:30
  5.9 0.5 collective-permute-start.2
  6.4 1.6 copy-done
  8.0 1.4 shard_map.17
  9.5 41.6 %collective-permute-done.refs_1_ = f32[512,1024]{1,0:T(8,128)S(1)} collective-permute-done((f32[512,1024]{1,0:T(8,128)}, f32[512,1024]{1,0:T(8,128)S(1)}, u32[]{:S(2)}, u32[]{:S(2)}) %collective-permute-start) | collective-permute-done | bytes 2097184 | tf_op jit(solution)/shard_map/ppermute | solution.py:30
  51.1 3.4 %collective-permute-done.1.refs_0_ = f32[512,1024]{1,0:T(8,128)} collective-permute-done((f32[512,1024]{1,0:T(8,128)}, f32[512,1024]{1,0:T(8,128)}, u32[]{:S(2)}, u32[]{:S(2)}) %collective-permute-start.1) | collective-permute-done | bytes 2097184 | tf_op jit(solution)/shard_map/ppermute | solution.py:30
  54.9 3.0 %collective-permute-start.3 = (f32[256,1024]{1,0:T(8,128)S(1)}, f32[256,1024]{1,0:T(8,128)S(1)}, u32[]{:S(2)}, u32[]{:S(2)}) collective-permute-start(f32[256,1024]{1,0:T(8,128)S(1)} %get-tuple-element.150), channel_id=1, source_target_pairs={{0,14},{1,15},{2,0},{3,1},{4,2},{5,3},{6,4},{7,5},{8,6},{9,7},{10,... | collective-permute-start | bytes 3145736 | tf_op jit(solution)/shard_map/ppermute | solution.py:30
  57.9 1.8 fusion.5
  59.8 3.4 %shard_map.18 = (bf16[512,1024]{1,0:T(8,128)(2,1)S(1)}, bf16[512,1024]{1,0:T(8,128)(2,1)S(1)}, bf16[512,1024]{1,0:T(8,128)(2,1)S(1)}, bf16[512,1024]{1,0:T(8,128...) custom-call(s32[4]{0:T(128)S(1)} %pad_add_fusion.place_ref, ...), custom_call_target="tpu_custom_call" | custom-call | tf_op jit(solution)/shard_map/pallas_call | solution.py:54
  63.3 8.7 %shard_map.19 = (f32[256,2048]{1,0:T(8,128)S(1)}, f32[256,2048]{1,0:T(8,128)S(1)}) custom-call(s32[4]{0:T(128)S(1)} %pad_add_fusion.place_ref, bf16[512,1024]{1,0:T(8,128)(2,1)S(1)} %get-tuple-element.85.refs_0_.refs_10_.refs_4_, bf16[512,1024]{1,0:T(8,128)(2,1)S(1)} %get-tuple-element.86.refs_1_.refs_11_.refs_5_, ...), custom_call_target="tpu_custom_call" | custom-call | tf_op jit(solution)/shard_map/pallas_call | solution.py:54
  72.0 6.9 %collective-permute-done.3.refs_2_ = f32[256,1024]{1,0:T(8,128)S(1)} collective-permute-done((f32[256,1024]{1,0:T(8,128)S(1)}, f32[256,1024]{1,0:T(8,128)S(1)}, u32[]{:S(2)}, u32[]{:S(2)}) %collective-permute-start.3) | collective-permute-done | bytes 1048608 | tf_op jit(solution)/shard_map/ppermute | solution.py:30
  78.9 5.3 %collective-permute-done.4.refs_0_ = f32[256,1024]{1,0:T(8,128)S(1)} collective-permute-done((f32[256,1024]{1,0:T(8,128)S(1)}, f32[256,1024]{1,0:T(8,128)S(1)}, u32[]{:S(2)}, u32[]{:S(2)}) %collective-permute-start.4) | collective-permute-done | bytes 1048608 | tf_op jit(solution)/shard_map/ppermute | solution.py:30
  84.2 2.0 %collective-permute-start.6 = (f32[256,1024]{1,0:T(8,128)S(1)}, f32[256,1024]{1,0:T(8,128)S(1)}, u32[]{:S(2)}, u32[]{:S(2)}) collective-permute-start(f32[256,1024]{1,0:T(8,128)S(1)} %get-tuple-element.96), channel_id=1, source_target_pairs={{0,2},{1,3},{2,4},{3,5},{4,6},{5,7},{6,8},{7,9},{8,10},{9,11},{10,... | collective-permute-start | bytes 3145736 | tf_op jit(solution)/shard_map/ppermute | solution.py:30
  86.7 1.6 collective-permute-done.8.got
  88.3 0.8 shard_map.20
  89.1 20.7 %collective-permute-done.5.refs_3_ = f32[256,1024]{1,0:T(8,128)S(1)} collective-permute-done((f32[256,1024]{1,0:T(8,128)S(1)}, f32[256,1024]{1,0:T(8,128)S(1)}, u32[]{:S(2)}, u32[]{:S(2)}) %collective-permute-start.5) | collective-permute-done | bytes 1048608 | tf_op jit(solution)/shard_map/ppermute | solution.py:30
  109.7 1.2 collective-permute-done.6.refs_1_
  110.9 1.8 collective-permute-done.7.refs_4_
  113.2 1.6 collective-permute-start.10
  114.8 1.7 collective-permute-start.11
  116.4 2.0 %collective-permute-start.12 = (f32[64,2048]{1,0:T(8,128)S(1)}, f32[64,2048]{1,0:T(8,128)S(1)}, u32[]{:S(2)}, u32[]{:S(2)}) collective-permute-start(f32[64,2048]{1,0:T(8,128)S(1)} %get-tuple-element.125), channel_id=1, source_target_pairs={{0,128},{1,129},{2,130},{3,131},{4,132},{5,133},{6,134},{7,135},{8... | collective-permute-start | bytes 1572872 | tf_op jit(solution)/shard_map/ppermute | solution.py:30
  118.6 1.6 shard_map.21
  120.2 8.7 %shard_map.22 = (f32[256,2048]{1,0:T(8,128)S(1)}, f32[256,2048]{1,0:T(8,128)S(1)}) custom-call(s32[4]{0:T(128)S(1)} %pad_add_fusion.place_ref, bf16[512,1024]{1,0:T(8,128)(2,1)S(1)} %get-tuple-element.108.refs_0_.refs_8_, bf16[512,1024]{1,0:T(8,128)(2,1)S(1)} %get-tuple-element.109.refs_1_.refs_9_, bf16[512,1024]{1,0:T(8,128)(2,1)S(1)} %get-tuple-element.110.refs_2_, ...), custom_call_target="tpu_custom_call" | custom-call | tf_op jit(solution)/shard_map/pallas_call | solution.py:54
  128.9 9.5 %collective-permute-done.9.refs_0_ = f32[256,1024]{1,0:T(8,128)S(1)} collective-permute-done((f32[256,1024]{1,0:T(8,128)S(1)}, f32[256,1024]{1,0:T(8,128)S(1)}, u32[]{:S(2)}, u32[]{:S(2)}) %collective-permute-start.9) | collective-permute-done | bytes 1048608 | tf_op jit(solution)/shard_map/ppermute | solution.py:30
  138.4 0.7 shard_map.23
  139.1 2.8 %shard_map.24 = (f32[256,2560]{1,0:T(8,128)S(1)}, f32[256,2560]{1,0:T(8,128)S(1)}) custom-call(s32[4]{0:T(128)S(1)} %pad_add_fusion.place_ref, bf16[512,1024]{1,0:T(8,128)(2,1)S(1)} %get-tuple-element.83.refs_6_.refs_0_, bf16[512,1024]{1,0:T(8,128)(2,1)S(1)} %get-tuple-element.84.refs_7_.refs_1_, bf16[256,1024]{1,0:T(8,128)(2,1)S(1)} %get-tuple-element.117.refs_2_, ...), custom_call_target="tpu_custom_call" | custom-call | tf_op jit(solution)/shard_map/pallas_call | solution.py:54
  142.0 4.9 %collective-permute-done.14.got = f32[256,2560]{1,0:T(8,128)S(1)} collective-permute-done((f32[256,2560]{1,0:T(8,128)S(1)}, f32[256,2560]{1,0:T(8,128)S(1)}, u32[]{:S(2)}, u32[]{:S(2)}) %collective-permute-start.14) | collective-permute-done | bytes 2621472 | tf_op jit(solution)/shard_map/ppermute | solution.py:30
  146.9 1.7 shard_map.26
  148.6 1.2 collective-permute-start.18
  149.8 1.6 collective-permute-start.15
  151.4 1.7 collective-permute-start.16
  153.1 2.0 %collective-permute-start.17 = (f32[64,1536]{1,0:T(8,128)}, f32[64,1536]{1,0:T(8,128)S(1)}, u32[]{:S(2)}, u32[]{:S(2)}) collective-permute-start(f32[64,1536]{1,0:T(8,128)} %get-tuple-element.138), channel_id=1, source_target_pairs={{0,128},{1,129},{2,130},{3,131},{4,132},{5,133},{6,134},{7,135},{8... | collective-permute-start | bytes 1179656 | tf_op jit(solution)/shard_map/ppermute | solution.py:30
  155.1 1.3 shard_map.25
  156.4 0.8 collective-permute-start.13
  157.2 11.1 %collective-permute-done.13 = f32[32,2048]{1,0:T(8,128)} collective-permute-done((f32[32,2048]{1,0:T(8,128)}, f32[32,2048]{1,0:T(8,128)}, u32[]{:S(2)}, u32[]{:S(2)}) %collective-permute-start.13) | collective-permute-done | bytes 262176 | tf_op jit(solution)/shard_map/ppermute | solution.py:30
  168.3 1.0 add.31
  169.3 1.9 collective-permute-start.21
  171.2 0.6 collective-permute-done.17.d
  171.8 0.7 shard_map.27
  172.5 1.2 collective-permute-start.22
  173.7 2.1 %collective-permute-start.23 = (f32[32,1024]{1,0:T(8,128)S(1)}, f32[32,1024]{1,0:T(8,128)S(1)}, u32[]{:S(2)}, u32[]{:S(2)}) collective-permute-start(f32[32,1024]{1,0:T(8,128)S(1)} %get-tuple-element.145), channel_id=1, source_target_pairs={{0,192},{1,193},{2,194},{3,195},{4,196},{5,197},{6,198},{7,199},{8... | collective-permute-start | bytes 393224 | tf_op jit(solution)/shard_map/ppermute | solution.py:30
  175.8 1.4 collective-permute-start.24
  177.2 1.2 collective-permute-start.19
  178.4 4.5 %collective-permute-done.19 = f32[32,1536]{1,0:T(8,128)S(1)} collective-permute-done((f32[32,1536]{1,0:T(8,128)S(1)}, f32[32,1536]{1,0:T(8,128)S(1)}, u32[]{:S(2)}, u32[]{:S(2)}) %collective-permute-start.19) | collective-permute-done | bytes 196640 | tf_op jit(solution)/shard_map/ppermute | solution.py:30
  183.1 1.2 collective-permute-start.25
  184.2 8.9 %collective-permute-done.20 = f32[32,1536]{1,0:T(8,128)S(1)} collective-permute-done((f32[32,1536]{1,0:T(8,128)S(1)}, f32[32,1536]{1,0:T(8,128)S(1)}, u32[]{:S(2)}, u32[]{:S(2)}) %collective-permute-start.20) | collective-permute-done | bytes 196640 | tf_op jit(solution)/shard_map/ppermute | solution.py:30
  193.2 1.0 collective-permute-done.25
  194.3 0.8 copy-done.1
  (36 shorter events, 2.1 us)
Async XLA Ops:
  0.0 51.1 %collective-permute-start = (f32[512,1024]{1,0:T(8,128)}, f32[512,1024]{1,0:T(8,128)S(1)}, u32[]{:S(2)}, u32[]{:S(2)}) collective-permute-start(f32[512,1024]{1,0:T(8,128)} %bitcast.34), channel_id=1, source_target_pairs={{0,14},{1,15},{2,0},{3,1},{4,2},{5,3},{6,4},{7,5},{8,6},{9,7},{10,... | collective-permute-start | bytes 6291464 | tf_op jit(solution)/shard_map/ppermute | solution.py:30
  5.9 48.6 %collective-permute-start.1 = (f32[512,1024]{1,0:T(8,128)}, f32[512,1024]{1,0:T(8,128)}, u32[]{:S(2)}, u32[]{:S(2)}) collective-permute-start(f32[512,1024]{1,0:T(8,128)} %bitcast.35), channel_id=1, source_target_pairs={{0,2},{1,3},{2,4},{3,5},{4,6},{5,7},{6,8},{7,9},{8,10},{9,11},{10,... | collective-permute-start | bytes 6291464 | tf_op jit(solution)/shard_map/ppermute | solution.py:30
  5.9 48.9 %collective-permute-start.2 = (f32[512,1024]{1,0:T(8,128)}, f32[512,1024]{1,0:T(8,128)}, u32[]{:S(2)}, u32[]{:S(2)}) collective-permute-start(f32[512,1024]{1,0:T(8,128)} %bitcast.36), channel_id=1, source_target_pairs={{0,1},{1,0},{2,3},{3,2},{4,5},{5,4},{6,7},{7,6},{8,9},{9,8},{10,11... | collective-permute-start | bytes 6291464 | tf_op jit(solution)/shard_map/ppermute | solution.py:30
  6.4 1.6 copy-start
  54.9 24.0 %collective-permute-start.3 = (f32[256,1024]{1,0:T(8,128)S(1)}, f32[256,1024]{1,0:T(8,128)S(1)}, u32[]{:S(2)}, u32[]{:S(2)}) collective-permute-start(f32[256,1024]{1,0:T(8,128)S(1)} %get-tuple-element.150), channel_id=1, source_target_pairs={{0,14},{1,15},{2,0},{3,1},{4,2},{5,3},{6,4},{7,5},{8,6},{9,7},{10,... | collective-permute-start | bytes 3145736 | tf_op jit(solution)/shard_map/ppermute | solution.py:30
  59.7 24.4 %collective-permute-start.4 = (f32[256,1024]{1,0:T(8,128)S(1)}, f32[256,1024]{1,0:T(8,128)S(1)}, u32[]{:S(2)}, u32[]{:S(2)}) collective-permute-start(f32[256,1024]{1,0:T(8,128)S(1)} %get-tuple-element.148), channel_id=1, source_target_pairs={{0,2},{1,3},{2,4},{3,5},{4,6},{5,7},{6,8},{7,9},{8,10},{9,11},{10,... | collective-permute-start | bytes 3145736 | tf_op jit(solution)/shard_map/ppermute | solution.py:30
  84.1 4.2 %collective-permute-start.8 = (f32[256,2048]{1,0:T(8,128)S(1)}, f32[256,2048]{1,0:T(8,128)S(1)}, u32[]{:S(2)}, u32[]{:S(2)}) collective-permute-start(f32[256,2048]{1,0:T(8,128)S(1)} %get-tuple-element.99), channel_id=1, source_target_pairs={{0,16},{1,17},{2,18},{3,19},{4,20},{5,21},{6,22},{7,23},{8,24},{9,... | collective-permute-start | bytes 6291464 | tf_op jit(solution)/shard_map/ppermute | solution.py:30
  84.2 25.6 %collective-permute-start.5 = (f32[256,1024]{1,0:T(8,128)S(1)}, f32[256,1024]{1,0:T(8,128)S(1)}, u32[]{:S(2)}, u32[]{:S(2)}) collective-permute-start(f32[256,1024]{1,0:T(8,128)S(1)} %get-tuple-element.95), channel_id=1, source_target_pairs={{0,14},{1,15},{2,0},{3,1},{4,2},{5,3},{6,4},{7,5},{8,6},{9,7},{10,... | collective-permute-start | bytes 3145736 | tf_op jit(solution)/shard_map/ppermute | solution.py:30
  84.2 26.8 %collective-permute-start.6 = (f32[256,1024]{1,0:T(8,128)S(1)}, f32[256,1024]{1,0:T(8,128)S(1)}, u32[]{:S(2)}, u32[]{:S(2)}) collective-permute-start(f32[256,1024]{1,0:T(8,128)S(1)} %get-tuple-element.96), channel_id=1, source_target_pairs={{0,2},{1,3},{2,4},{3,5},{4,6},{5,7},{6,8},{7,9},{8,10},{9,11},{10,... | collective-permute-start | bytes 3145736 | tf_op jit(solution)/shard_map/ppermute | solution.py:30
  86.2 26.5 %collective-permute-start.7 = (f32[256,1024]{1,0:T(8,128)S(1)}, f32[256,1024]{1,0:T(8,128)S(1)}, u32[]{:S(2)}, u32[]{:S(2)}) collective-permute-start(f32[256,1024]{1,0:T(8,128)S(1)} %collective-permute-done.3.refs_2_), channel_id=1, source_target_pairs={{0,1},{1,0},{2,3},{3,2},{4,5},{5,4},{6,7},{7,6},{8,9},{9,8},{10,11... | collective-permute-start | bytes 3145736 | tf_op jit(solution)/shard_map/ppermute | solution.py:30
  112.7 25.7 %collective-permute-start.9 = (f32[256,1024]{1,0:T(8,128)S(1)}, f32[256,1024]{1,0:T(8,128)S(1)}, u32[]{:S(2)}, u32[]{:S(2)}) collective-permute-start(f32[256,1024]{1,0:T(8,128)S(1)} %collective-permute-done.5.refs_3_), channel_id=1, source_target_pairs={{0,1},{1,0},{2,3},{3,2},{4,5},{5,4},{6,7},{7,6},{8,9},{9,8},{10,11... | collective-permute-start | bytes 3145736 | tf_op jit(solution)/shard_map/ppermute | solution.py:30
  113.2 28.7 %collective-permute-start.10 = (f32[64,2048]{1,0:T(8,128)S(1)}, f32[64,2048]{1,0:T(8,128)S(1)}, u32[]{:S(2)}, u32[]{:S(2)}) collective-permute-start(f32[64,2048]{1,0:T(8,128)S(1)} %get-tuple-element.124), channel_id=1, source_target_pairs={{0,64},{1,65},{2,66},{3,67},{4,68},{5,69},{6,70},{7,71},{8,72},{9,... | collective-permute-start | bytes 1572872 | tf_op jit(solution)/shard_map/ppermute | solution.py:30
  114.8 27.1 %collective-permute-start.11 = (f32[64,2048]{1,0:T(8,128)S(1)}, f32[64,2048]{1,0:T(8,128)S(1)}, u32[]{:S(2)}, u32[]{:S(2)}) collective-permute-start(f32[64,2048]{1,0:T(8,128)S(1)} %get-tuple-element.126), channel_id=1, source_target_pairs={{0,192},{1,193},{2,194},{3,195},{4,196},{5,197},{6,198},{7,199},{8... | collective-permute-start | bytes 1572872 | tf_op jit(solution)/shard_map/ppermute | solution.py:30
  116.4 25.5 %collective-permute-start.12 = (f32[64,2048]{1,0:T(8,128)S(1)}, f32[64,2048]{1,0:T(8,128)S(1)}, u32[]{:S(2)}, u32[]{:S(2)}) collective-permute-start(f32[64,2048]{1,0:T(8,128)S(1)} %get-tuple-element.125), channel_id=1, source_target_pairs={{0,128},{1,129},{2,130},{3,131},{4,132},{5,133},{6,134},{7,135},{8... | collective-permute-start | bytes 1572872 | tf_op jit(solution)/shard_map/ppermute | solution.py:30
  141.9 5.0 %collective-permute-start.14 = (f32[256,2560]{1,0:T(8,128)S(1)}, f32[256,2560]{1,0:T(8,128)S(1)}, u32[]{:S(2)}, u32[]{:S(2)}) collective-permute-start(f32[256,2560]{1,0:T(8,128)S(1)} %get-tuple-element.134), channel_id=1, source_target_pairs={{0,16},{1,17},{2,18},{3,19},{4,20},{5,21},{6,22},{7,23},{8,24},{9,... | collective-permute-start | bytes 7864328 | tf_op jit(solution)/shard_map/ppermute | solution.py:30
  148.6 23.2 %collective-permute-start.18 = (f32[128,1024]{1,0:T(8,128)S(1)}, f32[128,1024]{1,0:T(8,128)S(1)}, u32[]{:S(2)}, u32[]{:S(2)}) collective-permute-start(f32[128,1024]{1,0:T(8,128)S(1)} %get-tuple-element.140), channel_id=1, source_target_pairs={{0,32},{1,33},{2,34},{3,35},{4,36},{5,37},{6,38},{7,39},{8,40},{9,... | collective-permute-start | bytes 1572872 | tf_op jit(solution)/shard_map/ppermute | solution.py:30
  149.8 21.4 %collective-permute-start.15 = (f32[64,1536]{1,0:T(8,128)}, f32[64,1536]{1,0:T(8,128)S(1)}, u32[]{:S(2)}, u32[]{:S(2)}) collective-permute-start(f32[64,1536]{1,0:T(8,128)} %get-tuple-element.136), channel_id=1, source_target_pairs={{0,64},{1,65},{2,66},{3,67},{4,68},{5,69},{6,70},{7,71},{8,72},{9,... | collective-permute-start | bytes 1179656 | tf_op jit(solution)/shard_map/ppermute | solution.py:30
  151.4 19.8 %collective-permute-start.16 = (f32[64,1536]{1,0:T(8,128)}, f32[64,1536]{1,0:T(8,128)S(1)}, u32[]{:S(2)}, u32[]{:S(2)}) collective-permute-start(f32[64,1536]{1,0:T(8,128)} %get-tuple-element.137), channel_id=1, source_target_pairs={{0,192},{1,193},{2,194},{3,195},{4,196},{5,197},{6,198},{7,199},{8... | collective-permute-start | bytes 1179656 | tf_op jit(solution)/shard_map/ppermute | solution.py:30
  153.1 18.7 %collective-permute-start.17 = (f32[64,1536]{1,0:T(8,128)}, f32[64,1536]{1,0:T(8,128)S(1)}, u32[]{:S(2)}, u32[]{:S(2)}) collective-permute-start(f32[64,1536]{1,0:T(8,128)} %get-tuple-element.138), channel_id=1, source_target_pairs={{0,128},{1,129},{2,130},{3,131},{4,132},{5,133},{6,134},{7,135},{8... | collective-permute-start | bytes 1179656 | tf_op jit(solution)/shard_map/ppermute | solution.py:30
  156.4 11.9 %collective-permute-start.13 = (f32[32,2048]{1,0:T(8,128)}, f32[32,2048]{1,0:T(8,128)}, u32[]{:S(2)}, u32[]{:S(2)}) collective-permute-start(f32[32,2048]{1,0:T(8,128)} %get-tuple-element.132), channel_id=1, source_target_pairs={{0,32},{1,33},{2,34},{3,35},{4,36},{5,37},{6,38},{7,39},{8,40},{9,... | collective-permute-start | bytes 786440 | tf_op jit(solution)/shard_map/ppermute | solution.py:30
  169.3 14.9 %collective-permute-start.21 = (f32[32,1024]{1,0:T(8,128)S(1)}, f32[32,1024]{1,0:T(8,128)S(1)}, u32[]{:S(2)}, u32[]{:S(2)}) collective-permute-start(f32[32,1024]{1,0:T(8,128)S(1)} %slice.44), channel_id=1, source_target_pairs={{0,14},{1,15},{2,0},{3,1},{4,2},{5,3},{6,4},{7,5},{8,6},{9,7},{10,... | collective-permute-start | bytes 393224 | tf_op jit(solution)/shard_map/ppermute | solution.py:30
  172.5 10.5 %collective-permute-start.22 = (f32[32,1024]{1,0:T(8,128)S(1)}, f32[32,1024]{1,0:T(8,128)S(1)}, u32[]{:S(2)}, u32[]{:S(2)}) collective-permute-start(f32[32,1024]{1,0:T(8,128)S(1)} %get-tuple-element.144), channel_id=1, source_target_pairs={{0,64},{1,65},{2,66},{3,67},{4,68},{5,69},{6,70},{7,71},{8,72},{9,... | collective-permute-start | bytes 393224 | tf_op jit(solution)/shard_map/ppermute | solution.py:30
  173.7 9.3 %collective-permute-start.23 = (f32[32,1024]{1,0:T(8,128)S(1)}, f32[32,1024]{1,0:T(8,128)S(1)}, u32[]{:S(2)}, u32[]{:S(2)}) collective-permute-start(f32[32,1024]{1,0:T(8,128)S(1)} %get-tuple-element.145), channel_id=1, source_target_pairs={{0,192},{1,193},{2,194},{3,195},{4,196},{5,197},{6,198},{7,199},{8... | collective-permute-start | bytes 393224 | tf_op jit(solution)/shard_map/ppermute | solution.py:30
  175.8 7.2 %collective-permute-start.24 = (f32[32,1024]{1,0:T(8,128)S(1)}, f32[32,1024]{1,0:T(8,128)S(1)}, u32[]{:S(2)}, u32[]{:S(2)}) collective-permute-start(f32[32,1024]{1,0:T(8,128)S(1)} %get-tuple-element.146), channel_id=1, source_target_pairs={{0,128},{1,129},{2,130},{3,131},{4,132},{5,133},{6,134},{7,135},{8... | collective-permute-start | bytes 393224 | tf_op jit(solution)/shard_map/ppermute | solution.py:30
  177.2 5.7 %collective-permute-start.19 = (f32[32,1536]{1,0:T(8,128)S(1)}, f32[32,1536]{1,0:T(8,128)S(1)}, u32[]{:S(2)}, u32[]{:S(2)}) collective-permute-start(f32[32,1536]{1,0:T(8,128)S(1)} %get-tuple-element.142), channel_id=1, source_target_pairs={{0,32},{1,33},{2,34},{3,35},{4,36},{5,37},{6,38},{7,39},{8,40},{9,... | collective-permute-start | bytes 589832 | tf_op jit(solution)/shard_map/ppermute | solution.py:30
  182.9 10.2 %collective-permute-start.20 = (f32[32,1536]{1,0:T(8,128)S(1)}, f32[32,1536]{1,0:T(8,128)S(1)}, u32[]{:S(2)}, u32[]{:S(2)}) collective-permute-start(f32[32,1536]{1,0:T(8,128)S(1)} %add.32), channel_id=1, source_target_pairs={{0,12},{1,13},{2,14},{3,15},{4,0},{5,1},{6,2},{7,3},{8,4},{9,5},{1... | collective-permute-start | bytes 589832 | tf_op jit(solution)/shard_map/ppermute | solution.py:30
  183.1 11.1 %collective-permute-start.25 = (f32[32,1024]{1,0:T(8,128)S(1)}, f32[32,1024]{1,0:T(8,128)S(1)}, u32[]{:S(2)}, u32[]{:S(2)}) collective-permute-start(f32[32,1024]{1,0:T(8,128)S(1)} %add_add_fusion), channel_id=1, source_target_pairs={{0,14},{1,15},{2,0},{3,1},{4,2},{5,3},{6,4},{7,5},{8,6},{9,7},{10,... | collective-permute-start | bytes 393224 | tf_op jit(solution)/shard_map/ppermute | solution.py:30
  194.3 0.8 copy-start.1

commit v4 on v3

--- a/solution.py
+++ b/solution.py
@@ -214,11 +214,11 @@
     shapes = [(64, wide)] * NY + [(NY * SHARE, rest)] * NXL
     outs = call(kernel, shapes, [place_now, mine, send(other, swap_core)], 12)
     by_y, by_x = outs[:NY], outs[NY:]
-    got = [send(by_y[r], y_by(r)) for r in (1, 3, 2)] + [by_x[0], send(by_x[1], swap_xl)]
+    got = [send(by_y[r], y_by(r)) for r in (2, 1, 3)] + [by_x[0], send(by_x[1], swap_xl)]
     shapes = [(SHARE, wide)] * 2 + [(SHARE, rest)] * NY
     mine, other, *by_y = call(mixed_kernel, shapes, [place_now, by_y[0], *got], 8)
     first = mine + send(other, swap_xl)
-    got = [send(by_y[r], y_by(r)) for r in (1, 3, 2)]
+    got = [send(by_y[r], y_by(r)) for r in (2, 1, 3)]
     return first, by_y[0] + got[0] + got[1] + got[2]
 
 
@@ -252,11 +252,13 @@
 
     o2b = send(p2b, swap_xh)
     got1 = [send(parts1[r], y_by(r)) for r in (1, 3, 2)]
-    rows_m2, cols_p2, cols_o2a = split(place_now, [whole(m2a, m2b)], [whole(p2a, p2b), whole(o2a)])
+    rows_m2, rows_p2, cols_m2, cols_p2, cols_o2a = split(
+        place_now, [whole(m2a, m2b), whole(p2a, p2b)], [whole(m2a, m2b), whole(p2a, p2b), whole(o2a)]
+    )
     cols_o0a, cols_o0b = [[v[start:start + HALF] for v in cols_o0] for start in (0, HALF)]
     product2 = products(
         place_now,
-        [(rows_m2, cols_p2), (rows_m2, cols_o0), (rows_m1, cols_p2), (rows_m1, cols_o2a)],
+        [(rows_p2, cols_m2), (rows_m2, cols_o0), (rows_m1, cols_p2), (rows_m1, cols_o2a)],
         (),
         ((rows_own, tuple(cols_o0a)), (rows_m2, cols_o2a)),
     )
@@ -268,7 +270,8 @@
     product2, parts1, got1 = tie((product2, parts1, got1))
     far, v = mixed_sum(place_now, *product2, (0, 1, 2, 3, 7, 9), (4, 5, 6, 8))
     x = far[:, 1024:]
-    d4, t2, far = jnp.split(send(far, z_by(-2)), 3, 1)
+    d4 = send(far[:, :512], z_by(2))
+    t2, far = jnp.split(send(far[:, 512:], z_by(-2)), 2, 1)
     d3, t3 = jnp.split(send(v, z_by(-1)), 2, 1)
     x = jnp.where(first, x, far)
 

time: 196 us -> 194 us (0.990)
  waiting for transfers between devices: 123 us -> 115 us
  starting transfers between devices: 34.1 us -> 39.6 us
    ppermute x26 -> x27, waiting for transfers between devices: 123 us -> 115 us  [send(): return lax.ppermute(value, ('aux', 'bas'), pairs)]
    ppermute x26 -> x27, starting transfers between devices: 34.1 us -> 39.6 us  [send(): return lax.ppermute(value, ('aux', 'bas'), pairs)]
  transfers between devices with their start and end apart: 26 -> 27, of which waited for: 16 -> 15; matrix products, arithmetic and copies ran while one was open for 2% -> 2% of each run, Pallas kernels for 15% -> 16%
where the time goes in v4:
time: 194 us
  waiting for transfers between devices  115 us (59%)
  starting transfers between devices  39.6 us (20%)
  Pallas kernels  32.7 us (17%)
  local copies, waits for them, and re-layouts  4.55 us (2%)
    ppermute x27, waiting for transfers between devices, send(): return lax.ppermute(value, ('aux', 'bas'), pairs)  115 us
    ppermute x27, starting transfers between devices, send(): return lax.ppermute(value, ('aux', 'bas'), pairs)  39.6 us
    pallas_call x11, Pallas kernels, call(): pl.pallas_call(kernel, out_shape=[jax.ShapeDtypeStruct(shape, dtype) for...  32.7 us
  transfers between devices with their start and end apart: 27, of which 15 were waited for; matrix products, arithmetic and copies ran while one was open for 2% of the time, Pallas kernels for 16%

profile of v4, /device:TPU:4, one launch (start us, length us, event | category | flops | bytes accessed | tf_op | source)
XLA Modules:
  0.0 193.8 jit_solution(6925064930570924498)
XLA Ops:
  0.0 5.9 %collective-permute-start = (f32[512,1024]{1,0:T(8,128)}, f32[512,1024]{1,0:T(8,128)S(1)}, u32[]{:S(2)}, u32[]{:S(2)}) collective-permute-start(f32[512,1024]{1,0:T(8,128)} %bitcast.32), channel_id=1, source_target_pairs={{0,14},{1,15},{2,0},{3,1},{4,2},{5,3},{6,4},{7,5},{8,6},{9,7},{10,... | collective-permute-start | bytes 6291464 | tf_op jit(solution)/shard_map/ppermute | solution.py:30
  5.9 0.5 collective-permute-start.2
  6.4 1.6 copy-done
  8.0 1.4 shard_map.17
  9.5 41.6 %collective-permute-done.refs_1_ = f32[512,1024]{1,0:T(8,128)S(1)} collective-permute-done((f32[512,1024]{1,0:T(8,128)}, f32[512,1024]{1,0:T(8,128)S(1)}, u32[]{:S(2)}, u32[]{:S(2)}) %collective-permute-start) | collective-permute-done | bytes 2097184 | tf_op jit(solution)/shard_map/ppermute | solution.py:30
  51.1 3.4 %collective-permute-done.1.refs_0_ = f32[512,1024]{1,0:T(8,128)} collective-permute-done((f32[512,1024]{1,0:T(8,128)}, f32[512,1024]{1,0:T(8,128)}, u32[]{:S(2)}, u32[]{:S(2)}) %collective-permute-start.1) | collective-permute-done | bytes 2097184 | tf_op jit(solution)/shard_map/ppermute | solution.py:30
  54.9 3.0 %collective-permute-start.3 = (f32[256,1024]{1,0:T(8,128)S(1)}, f32[256,1024]{1,0:T(8,128)S(1)}, u32[]{:S(2)}, u32[]{:S(2)}) collective-permute-start(f32[256,1024]{1,0:T(8,128)S(1)} %get-tuple-element.158), channel_id=1, source_target_pairs={{0,14},{1,15},{2,0},{3,1},{4,2},{5,3},{6,4},{7,5},{8,6},{9,7},{10,... | collective-permute-start | bytes 3145736 | tf_op jit(solution)/shard_map/ppermute | solution.py:30
  57.9 1.8 fusion.4
  59.8 3.4 %shard_map.18 = (bf16[512,1024]{1,0:T(8,128)(2,1)S(1)}, bf16[512,1024]{1,0:T(8,128)(2,1)S(1)}, bf16[512,1024]{1,0:T(8,128)(2,1)S(1)}, bf16[512,1024]{1,0:T(8,128...) custom-call(s32[4]{0:T(128)S(1)} %pad_add_fusion.place_ref, ...), custom_call_target="tpu_custom_call" | custom-call | tf_op jit(solution)/shard_map/pallas_call | solution.py:54
  63.3 8.7 %shard_map.19 = (f32[256,2048]{1,0:T(8,128)S(1)}, f32[256,2048]{1,0:T(8,128)S(1)}) custom-call(s32[4]{0:T(128)S(1)} %pad_add_fusion.place_ref, bf16[512,1024]{1,0:T(8,128)(2,1)S(1)} %get-tuple-element.89.refs_0_.refs_14_.refs_4_, bf16[512,1024]{1,0:T(8,128)(2,1)S(1)} %get-tuple-element.90.refs_1_.refs_15_.refs_5_, ...), custom_call_target="tpu_custom_call" | custom-call | tf_op jit(solution)/shard_map/pallas_call | solution.py:54
  72.0 6.9 %collective-permute-done.3.refs_2_ = f32[256,1024]{1,0:T(8,128)S(1)} collective-permute-done((f32[256,1024]{1,0:T(8,128)S(1)}, f32[256,1024]{1,0:T(8,128)S(1)}, u32[]{:S(2)}, u32[]{:S(2)}) %collective-permute-start.3) | collective-permute-done | bytes 1048608 | tf_op jit(solution)/shard_map/ppermute | solution.py:30
  78.9 5.3 %collective-permute-done.4.refs_0_ = f32[256,1024]{1,0:T(8,128)S(1)} collective-permute-done((f32[256,1024]{1,0:T(8,128)S(1)}, f32[256,1024]{1,0:T(8,128)S(1)}, u32[]{:S(2)}, u32[]{:S(2)}) %collective-permute-start.4) | collective-permute-done | bytes 1048608 | tf_op jit(solution)/shard_map/ppermute | solution.py:30
  84.2 2.0 %collective-permute-start.6 = (f32[256,1024]{1,0:T(8,128)S(1)}, f32[256,1024]{1,0:T(8,128)S(1)}, u32[]{:S(2)}, u32[]{:S(2)}) collective-permute-start(f32[256,1024]{1,0:T(8,128)S(1)} %get-tuple-element.100), channel_id=1, source_target_pairs={{0,2},{1,3},{2,4},{3,5},{4,6},{5,7},{6,8},{7,9},{8,10},{9,11},{10,... | collective-permute-start | bytes 3145736 | tf_op jit(solution)/shard_map/ppermute | solution.py:30
  86.7 1.6 collective-permute-done.8.got
  88.3 0.8 shard_map.20
  89.1 20.7 %collective-permute-done.5.refs_3_ = f32[256,1024]{1,0:T(8,128)S(1)} collective-permute-done((f32[256,1024]{1,0:T(8,128)S(1)}, f32[256,1024]{1,0:T(8,128)S(1)}, u32[]{:S(2)}, u32[]{:S(2)}) %collective-permute-start.5) | collective-permute-done | bytes 1048608 | tf_op jit(solution)/shard_map/ppermute | solution.py:30
  109.7 1.2 collective-permute-done.6.refs_1_
  110.9 1.8 collective-permute-done.7.refs_4_
  113.2 1.6 collective-permute-start.10
  114.8 1.7 collective-permute-start.11
  116.4 2.0 %collective-permute-start.12 = (f32[64,2048]{1,0:T(8,128)S(1)}, f32[64,2048]{1,0:T(8,128)S(1)}, u32[]{:S(2)}, u32[]{:S(2)}) collective-permute-start(f32[64,2048]{1,0:T(8,128)S(1)} %get-tuple-element.133), channel_id=1, source_target_pairs={{0,128},{1,129},{2,130},{3,131},{4,132},{5,133},{6,134},{7,135},{8... | collective-permute-start | bytes 1572872 | tf_op jit(solution)/shard_map/ppermute | solution.py:30
  118.6 2.5 %shard_map.21 = (bf16[512,1024]{1,0:T(8,128)(2,1)S(1)}, bf16[512,1024]{1,0:T(8,128)(2,1)S(1)}, bf16[512,1024]{1,0:T(8,128)(2,1)S(1)}, bf16[512,1024]{1,0:T(8,128...) custom-call(s32[4]{0:T(128)S(1)} %pad_add_fusion.place_ref, ...), custom_call_target="tpu_custom_call" | custom-call | tf_op jit(solution)/shard_map/pallas_call | solution.py:54
  121.1 8.7 %shard_map.22 = (f32[256,2048]{1,0:T(8,128)S(1)}, f32[256,2048]{1,0:T(8,128)S(1)}) custom-call(s32[4]{0:T(128)S(1)} %pad_add_fusion.place_ref, bf16[512,1024]{1,0:T(8,128)(2,1)S(1)} %get-tuple-element.112.refs_0_, bf16[512,1024]{1,0:T(8,128)(2,1)S(1)} %get-tuple-element.113.refs_1_, bf16[512,1024]{1,0:T(8,128)(2,1)S(1)} %get-tuple-element.114.refs_2_, ...), custom_call_target="tpu_custom_call" | custom-call | tf_op jit(solution)/shard_map/pallas_call | solution.py:54
  129.8 8.6 %collective-permute-done.9.refs_0_ = f32[256,1024]{1,0:T(8,128)S(1)} collective-permute-done((f32[256,1024]{1,0:T(8,128)S(1)}, f32[256,1024]{1,0:T(8,128)S(1)}, u32[]{:S(2)}, u32[]{:S(2)}) %collective-permute-start.9) | collective-permute-done | bytes 1048608 | tf_op jit(solution)/shard_map/ppermute | solution.py:30
  138.4 0.7 shard_map.23
  139.1 2.8 %shard_map.24 = (f32[256,2560]{1,0:T(8,128)S(1)}, f32[256,2560]{1,0:T(8,128)S(1)}) custom-call(s32[4]{0:T(128)S(1)} %pad_add_fusion.place_ref, bf16[512,1024]{1,0:T(8,128)(2,1)S(1)} %get-tuple-element.87.refs_6_.refs_8_.refs_0_, bf16[512,1024]{1,0:T(8,128)(2,1)S(1)} %get-tuple-element.88.refs_7_.refs_9_.refs_1_, ...), custom_call_target="tpu_custom_call" | custom-call | tf_op jit(solution)/shard_map/pallas_call | solution.py:54
  142.0 4.9 %collective-permute-done.14.got = f32[256,2560]{1,0:T(8,128)S(1)} collective-permute-done((f32[256,2560]{1,0:T(8,128)S(1)}, f32[256,2560]{1,0:T(8,128)S(1)}, u32[]{:S(2)}, u32[]{:S(2)}) %collective-permute-start.14) | collective-permute-done | bytes 2621472 | tf_op jit(solution)/shard_map/ppermute | solution.py:30
  146.9 1.7 shard_map.26
  148.6 1.2 collective-permute-start.18
  149.8 3.2 %collective-permute-start.15 = (f32[64,1536]{1,0:T(8,128)}, f32[64,1536]{1,0:T(8,128)S(1)}, u32[]{:S(2)}, u32[]{:S(2)}) collective-permute-start(f32[64,1536]{1,0:T(8,128)} %get-tuple-element.144), channel_id=1, source_target_pairs={{0,128},{1,129},{2,130},{3,131},{4,132},{5,133},{6,134},{7,135},{8... | collective-permute-start | bytes 1179656 | tf_op jit(solution)/shard_map/ppermute | solution.py:30
  153.0 0.7 collective-permute-start.16
  153.7 2.6 %collective-permute-start.17 = (f32[64,1536]{1,0:T(8,128)}, f32[64,1536]{1,0:T(8,128)S(1)}, u32[]{:S(2)}, u32[]{:S(2)}) collective-permute-start(f32[64,1536]{1,0:T(8,128)} %get-tuple-element.146), channel_id=1, source_target_pairs={{0,192},{1,193},{2,194},{3,195},{4,196},{5,197},{6,198},{7,199},{8... | collective-permute-start | bytes 1179656 | tf_op jit(solution)/shard_map/ppermute | solution.py:30
  156.3 1.3 shard_map.25
  157.6 0.8 collective-permute-start.13
  158.4 9.9 %collective-permute-done.13 = f32[32,2048]{1,0:T(8,128)} collective-permute-done((f32[32,2048]{1,0:T(8,128)}, f32[32,2048]{1,0:T(8,128)}, u32[]{:S(2)}, u32[]{:S(2)}) %collective-permute-start.13) | collective-permute-done | bytes 262176 | tf_op jit(solution)/shard_map/ppermute | solution.py:30
  168.3 1.0 add.31
  169.3 1.9 collective-permute-start.21
  171.3 0.7 shard_map.27
  171.9 3.3 %collective-permute-start.22 = (f32[32,1024]{1,0:T(8,128)S(1)}, f32[32,1024]{1,0:T(8,128)S(1)}, u32[]{:S(2)}, u32[]{:S(2)}) collective-permute-start(f32[32,1024]{1,0:T(8,128)S(1)} %get-tuple-element.152), channel_id=1, source_target_pairs={{0,128},{1,129},{2,130},{3,131},{4,132},{5,133},{6,134},{7,135},{8... | collective-permute-start | bytes 393224 | tf_op jit(solution)/shard_map/ppermute | solution.py:30
  175.2 0.7 collective-permute-start.23
  175.9 2.6 %collective-permute-start.24 = (f32[32,1024]{1,0:T(8,128)S(1)}, f32[32,1024]{1,0:T(8,128)S(1)}, u32[]{:S(2)}, u32[]{:S(2)}) collective-permute-start(f32[32,1024]{1,0:T(8,128)S(1)} %get-tuple-element.154), channel_id=1, source_target_pairs={{0,192},{1,193},{2,194},{3,195},{4,196},{5,197},{6,198},{7,199},{8... | collective-permute-start | bytes 393224 | tf_op jit(solution)/shard_map/ppermute | solution.py:30
  178.4 1.2 collective-permute-start.19
  179.6 4.5 %collective-permute-done.19 = f32[32,1536]{1,0:T(8,128)S(1)} collective-permute-done((f32[32,1536]{1,0:T(8,128)S(1)}, f32[32,1536]{1,0:T(8,128)S(1)}, u32[]{:S(2)}, u32[]{:S(2)}) %collective-permute-start.19) | collective-permute-done | bytes 196640 | tf_op jit(solution)/shard_map/ppermute | solution.py:30
  184.3 1.2 collective-permute-start.25
  185.5 2.5 %collective-permute-start.26 = (f32[32,512]{1,0:T(8,128)S(1)}, f32[32,512]{1,0:T(8,128)S(1)}, u32[]{:S(2)}, u32[]{:S(2)}) collective-permute-start(f32[32,512]{1,0:T(8,128)S(1)} %slice.54), channel_id=1, source_target_pairs={{0,4},{1,5},{2,6},{3,7},{4,8},{5,9},{6,10},{7,11},{8,12},{9,13},{1... | collective-permute-start | bytes 196616 | tf_op jit(solution)/shard_map/ppermute | solution.py:30
  187.9 3.8 %collective-permute-done.20 = f32[32,1024]{1,0:T(8,128)S(1)} collective-permute-done((f32[32,1024]{1,0:T(8,128)S(1)}, f32[32,1024]{1,0:T(8,128)S(1)}, u32[]{:S(2)}, u32[]{:S(2)}) %collective-permute-start.20) | collective-permute-done | bytes 131104 | tf_op jit(solution)/shard_map/ppermute | solution.py:30
  191.9 1.0 collective-permute-done.25
  193.0 0.8 copy-done.1
  (40 shorter events, 2.2 us)
Async XLA Ops:
  0.0 51.1 %collective-permute-start = (f32[512,1024]{1,0:T(8,128)}, f32[512,1024]{1,0:T(8,128)S(1)}, u32[]{:S(2)}, u32[]{:S(2)}) collective-permute-start(f32[512,1024]{1,0:T(8,128)} %bitcast.32), channel_id=1, source_target_pairs={{0,14},{1,15},{2,0},{3,1},{4,2},{5,3},{6,4},{7,5},{8,6},{9,7},{10,... | collective-permute-start | bytes 6291464 | tf_op jit(solution)/shard_map/ppermute | solution.py:30
  5.9 48.6 %collective-permute-start.1 = (f32[512,1024]{1,0:T(8,128)}, f32[512,1024]{1,0:T(8,128)}, u32[]{:S(2)}, u32[]{:S(2)}) collective-permute-start(f32[512,1024]{1,0:T(8,128)} %bitcast.33), channel_id=1, source_target_pairs={{0,2},{1,3},{2,4},{3,5},{4,6},{5,7},{6,8},{7,9},{8,10},{9,11},{10,... | collective-permute-start | bytes 6291464 | tf_op jit(solution)/shard_map/ppermute | solution.py:30
  5.9 48.9 %collective-permute-start.2 = (f32[512,1024]{1,0:T(8,128)}, f32[512,1024]{1,0:T(8,128)}, u32[]{:S(2)}, u32[]{:S(2)}) collective-permute-start(f32[512,1024]{1,0:T(8,128)} %bitcast.34), channel_id=1, source_target_pairs={{0,1},{1,0},{2,3},{3,2},{4,5},{5,4},{6,7},{7,6},{8,9},{9,8},{10,11... | collective-permute-start | bytes 6291464 | tf_op jit(solution)/shard_map/ppermute | solution.py:30
  6.4 1.6 copy-start
  54.9 24.0 %collective-permute-start.3 = (f32[256,1024]{1,0:T(8,128)S(1)}, f32[256,1024]{1,0:T(8,128)S(1)}, u32[]{:S(2)}, u32[]{:S(2)}) collective-permute-start(f32[256,1024]{1,0:T(8,128)S(1)} %get-tuple-element.158), channel_id=1, source_target_pairs={{0,14},{1,15},{2,0},{3,1},{4,2},{5,3},{6,4},{7,5},{8,6},{9,7},{10,... | collective-permute-start | bytes 3145736 | tf_op jit(solution)/shard_map/ppermute | solution.py:30
  59.7 24.4 %collective-permute-start.4 = (f32[256,1024]{1,0:T(8,128)S(1)}, f32[256,1024]{1,0:T(8,128)S(1)}, u32[]{:S(2)}, u32[]{:S(2)}) collective-permute-start(f32[256,1024]{1,0:T(8,128)S(1)} %get-tuple-element.156), channel_id=1, source_target_pairs={{0,2},{1,3},{2,4},{3,5},{4,6},{5,7},{6,8},{7,9},{8,10},{9,11},{10,... | collective-permute-start | bytes 3145736 | tf_op jit(solution)/shard_map/ppermute | solution.py:30
  84.1 4.2 %collective-permute-start.8 = (f32[256,2048]{1,0:T(8,128)S(1)}, f32[256,2048]{1,0:T(8,128)S(1)}, u32[]{:S(2)}, u32[]{:S(2)}) collective-permute-start(f32[256,2048]{1,0:T(8,128)S(1)} %get-tuple-element.103), channel_id=1, source_target_pairs={{0,16},{1,17},{2,18},{3,19},{4,20},{5,21},{6,22},{7,23},{8,24},{9,... | collective-permute-start | bytes 6291464 | tf_op jit(solution)/shard_map/ppermute | solution.py:30
  84.2 25.6 %collective-permute-start.5 = (f32[256,1024]{1,0:T(8,128)S(1)}, f32[256,1024]{1,0:T(8,128)S(1)}, u32[]{:S(2)}, u32[]{:S(2)}) collective-permute-start(f32[256,1024]{1,0:T(8,128)S(1)} %get-tuple-element.99), channel_id=1, source_target_pairs={{0,14},{1,15},{2,0},{3,1},{4,2},{5,3},{6,4},{7,5},{8,6},{9,7},{10,... | collective-permute-start | bytes 3145736 | tf_op jit(solution)/shard_map/ppermute | solution.py:30
  84.2 26.8 %collective-permute-start.6 = (f32[256,1024]{1,0:T(8,128)S(1)}, f32[256,1024]{1,0:T(8,128)S(1)}, u32[]{:S(2)}, u32[]{:S(2)}) collective-permute-start(f32[256,1024]{1,0:T(8,128)S(1)} %get-tuple-element.100), channel_id=1, source_target_pairs={{0,2},{1,3},{2,4},{3,5},{4,6},{5,7},{6,8},{7,9},{8,10},{9,11},{10,... | collective-permute-start | bytes 3145736 | tf_op jit(solution)/shard_map/ppermute | solution.py:30
  86.2 26.5 %collective-permute-start.7 = (f32[256,1024]{1,0:T(8,128)S(1)}, f32[256,1024]{1,0:T(8,128)S(1)}, u32[]{:S(2)}, u32[]{:S(2)}) collective-permute-start(f32[256,1024]{1,0:T(8,128)S(1)} %collective-permute-done.3.refs_2_), channel_id=1, source_target_pairs={{0,1},{1,0},{2,3},{3,2},{4,5},{5,4},{6,7},{7,6},{8,9},{9,8},{10,11... | collective-permute-start | bytes 3145736 | tf_op jit(solution)/shard_map/ppermute | solution.py:30
  112.7 25.7 %collective-permute-start.9 = (f32[256,1024]{1,0:T(8,128)S(1)}, f32[256,1024]{1,0:T(8,128)S(1)}, u32[]{:S(2)}, u32[]{:S(2)}) collective-permute-start(f32[256,1024]{1,0:T(8,128)S(1)} %collective-permute-done.5.refs_3_), channel_id=1, source_target_pairs={{0,1},{1,0},{2,3},{3,2},{4,5},{5,4},{6,7},{7,6},{8,9},{9,8},{10,11... | collective-permute-start | bytes 3145736 | tf_op jit(solution)/shard_map/ppermute | solution.py:30
  113.2 28.7 %collective-permute-start.10 = (f32[64,2048]{1,0:T(8,128)S(1)}, f32[64,2048]{1,0:T(8,128)S(1)}, u32[]{:S(2)}, u32[]{:S(2)}) collective-permute-start(f32[64,2048]{1,0:T(8,128)S(1)} %get-tuple-element.132), channel_id=1, source_target_pairs={{0,64},{1,65},{2,66},{3,67},{4,68},{5,69},{6,70},{7,71},{8,72},{9,... | collective-permute-start | bytes 1572872 | tf_op jit(solution)/shard_map/ppermute | solution.py:30
  114.8 27.1 %collective-permute-start.11 = (f32[64,2048]{1,0:T(8,128)S(1)}, f32[64,2048]{1,0:T(8,128)S(1)}, u32[]{:S(2)}, u32[]{:S(2)}) collective-permute-start(f32[64,2048]{1,0:T(8,128)S(1)} %get-tuple-element.134), channel_id=1, source_target_pairs={{0,192},{1,193},{2,194},{3,195},{4,196},{5,197},{6,198},{7,199},{8... | collective-permute-start | bytes 1572872 | tf_op jit(solution)/shard_map/ppermute | solution.py:30
  116.4 25.5 %collective-permute-start.12 = (f32[64,2048]{1,0:T(8,128)S(1)}, f32[64,2048]{1,0:T(8,128)S(1)}, u32[]{:S(2)}, u32[]{:S(2)}) collective-permute-start(f32[64,2048]{1,0:T(8,128)S(1)} %get-tuple-element.133), channel_id=1, source_target_pairs={{0,128},{1,129},{2,130},{3,131},{4,132},{5,133},{6,134},{7,135},{8... | collective-permute-start | bytes 1572872 | tf_op jit(solution)/shard_map/ppermute | solution.py:30
  141.9 5.0 %collective-permute-start.14 = (f32[256,2560]{1,0:T(8,128)S(1)}, f32[256,2560]{1,0:T(8,128)S(1)}, u32[]{:S(2)}, u32[]{:S(2)}) collective-permute-start(f32[256,2560]{1,0:T(8,128)S(1)} %get-tuple-element.142), channel_id=1, source_target_pairs={{0,16},{1,17},{2,18},{3,19},{4,20},{5,21},{6,22},{7,23},{8,24},{9,... | collective-permute-start | bytes 7864328 | tf_op jit(solution)/shard_map/ppermute | solution.py:30
  148.6 22.6 %collective-permute-start.18 = (f32[128,1024]{1,0:T(8,128)S(1)}, f32[128,1024]{1,0:T(8,128)S(1)}, u32[]{:S(2)}, u32[]{:S(2)}) collective-permute-start(f32[128,1024]{1,0:T(8,128)S(1)} %get-tuple-element.148), channel_id=1, source_target_pairs={{0,32},{1,33},{2,34},{3,35},{4,36},{5,37},{6,38},{7,39},{8,40},{9,... | collective-permute-start | bytes 1572872 | tf_op jit(solution)/shard_map/ppermute | solution.py:30
  149.8 21.4 %collective-permute-start.15 = (f32[64,1536]{1,0:T(8,128)}, f32[64,1536]{1,0:T(8,128)S(1)}, u32[]{:S(2)}, u32[]{:S(2)}) collective-permute-start(f32[64,1536]{1,0:T(8,128)} %get-tuple-element.144), channel_id=1, source_target_pairs={{0,128},{1,129},{2,130},{3,131},{4,132},{5,133},{6,134},{7,135},{8... | collective-permute-start | bytes 1179656 | tf_op jit(solution)/shard_map/ppermute | solution.py:30
  153.0 18.2 %collective-permute-start.16 = (f32[64,1536]{1,0:T(8,128)}, f32[64,1536]{1,0:T(8,128)S(1)}, u32[]{:S(2)}, u32[]{:S(2)}) collective-permute-start(f32[64,1536]{1,0:T(8,128)} %get-tuple-element.145), channel_id=1, source_target_pairs={{0,64},{1,65},{2,66},{3,67},{4,68},{5,69},{6,70},{7,71},{8,72},{9,... | collective-permute-start | bytes 1179656 | tf_op jit(solution)/shard_map/ppermute | solution.py:30
  153.7 17.5 %collective-permute-start.17 = (f32[64,1536]{1,0:T(8,128)}, f32[64,1536]{1,0:T(8,128)S(1)}, u32[]{:S(2)}, u32[]{:S(2)}) collective-permute-start(f32[64,1536]{1,0:T(8,128)} %get-tuple-element.146), channel_id=1, source_target_pairs={{0,192},{1,193},{2,194},{3,195},{4,196},{5,197},{6,198},{7,199},{8... | collective-permute-start | bytes 1179656 | tf_op jit(solution)/shard_map/ppermute | solution.py:30
  157.6 10.7 %collective-permute-start.13 = (f32[32,2048]{1,0:T(8,128)}, f32[32,2048]{1,0:T(8,128)}, u32[]{:S(2)}, u32[]{:S(2)}) collective-permute-start(f32[32,2048]{1,0:T(8,128)} %get-tuple-element.140), channel_id=1, source_target_pairs={{0,32},{1,33},{2,34},{3,35},{4,36},{5,37},{6,38},{7,39},{8,40},{9,... | collective-permute-start | bytes 786440 | tf_op jit(solution)/shard_map/ppermute | solution.py:30
  169.3 18.6 %collective-permute-start.21 = (f32[32,1024]{1,0:T(8,128)S(1)}, f32[32,1024]{1,0:T(8,128)S(1)}, u32[]{:S(2)}, u32[]{:S(2)}) collective-permute-start(f32[32,1024]{1,0:T(8,128)S(1)} %slice.53), channel_id=1, source_target_pairs={{0,14},{1,15},{2,0},{3,1},{4,2},{5,3},{6,4},{7,5},{8,6},{9,7},{10,... | collective-permute-start | bytes 393224 | tf_op jit(solution)/shard_map/ppermute | solution.py:30
  171.9 12.3 %collective-permute-start.22 = (f32[32,1024]{1,0:T(8,128)S(1)}, f32[32,1024]{1,0:T(8,128)S(1)}, u32[]{:S(2)}, u32[]{:S(2)}) collective-permute-start(f32[32,1024]{1,0:T(8,128)S(1)} %get-tuple-element.152), channel_id=1, source_target_pairs={{0,128},{1,129},{2,130},{3,131},{4,132},{5,133},{6,134},{7,135},{8... | collective-permute-start | bytes 393224 | tf_op jit(solution)/shard_map/ppermute | solution.py:30
  175.2 9.1 %collective-permute-start.23 = (f32[32,1024]{1,0:T(8,128)S(1)}, f32[32,1024]{1,0:T(8,128)S(1)}, u32[]{:S(2)}, u32[]{:S(2)}) collective-permute-start(f32[32,1024]{1,0:T(8,128)S(1)} %get-tuple-element.153), channel_id=1, source_target_pairs={{0,64},{1,65},{2,66},{3,67},{4,68},{5,69},{6,70},{7,71},{8,72},{9,... | collective-permute-start | bytes 393224 | tf_op jit(solution)/shard_map/ppermute | solution.py:30
  175.9 8.4 %collective-permute-start.24 = (f32[32,1024]{1,0:T(8,128)S(1)}, f32[32,1024]{1,0:T(8,128)S(1)}, u32[]{:S(2)}, u32[]{:S(2)}) collective-permute-start(f32[32,1024]{1,0:T(8,128)S(1)} %get-tuple-element.154), channel_id=1, source_target_pairs={{0,192},{1,193},{2,194},{3,195},{4,196},{5,197},{6,198},{7,199},{8... | collective-permute-start | bytes 393224 | tf_op jit(solution)/shard_map/ppermute | solution.py:30
  178.4 5.7 %collective-permute-start.19 = (f32[32,1536]{1,0:T(8,128)S(1)}, f32[32,1536]{1,0:T(8,128)S(1)}, u32[]{:S(2)}, u32[]{:S(2)}) collective-permute-start(f32[32,1536]{1,0:T(8,128)S(1)} %get-tuple-element.150), channel_id=1, source_target_pairs={{0,32},{1,33},{2,34},{3,35},{4,36},{5,37},{6,38},{7,39},{8,40},{9,... | collective-permute-start | bytes 589832 | tf_op jit(solution)/shard_map/ppermute | solution.py:30
  184.2 7.6 %collective-permute-start.20 = (f32[32,1024]{1,0:T(8,128)S(1)}, f32[32,1024]{1,0:T(8,128)S(1)}, u32[]{:S(2)}, u32[]{:S(2)}) collective-permute-start(f32[32,1024]{1,0:T(8,128)S(1)} %slice.52), channel_id=1, source_target_pairs={{0,12},{1,13},{2,14},{3,15},{4,0},{5,1},{6,2},{7,3},{8,4},{9,5},{1... | collective-permute-start | bytes 393224 | tf_op jit(solution)/shard_map/ppermute | solution.py:30
  184.3 8.6 %collective-permute-start.25 = (f32[32,1024]{1,0:T(8,128)S(1)}, f32[32,1024]{1,0:T(8,128)S(1)}, u32[]{:S(2)}, u32[]{:S(2)}) collective-permute-start(f32[32,1024]{1,0:T(8,128)S(1)} %add_add_fusion), channel_id=1, source_target_pairs={{0,14},{1,15},{2,0},{3,1},{4,2},{5,3},{6,4},{7,5},{8,6},{9,7},{10,... | collective-permute-start | bytes 393224 | tf_op jit(solution)/shard_map/ppermute | solution.py:30
  185.5 7.5 %collective-permute-start.26 = (f32[32,512]{1,0:T(8,128)S(1)}, f32[32,512]{1,0:T(8,128)S(1)}, u32[]{:S(2)}, u32[]{:S(2)}) collective-permute-start(f32[32,512]{1,0:T(8,128)S(1)} %slice.54), channel_id=1, source_target_pairs={{0,4},{1,5},{2,6},{3,7},{4,8},{5,9},{6,10},{7,11},{8,12},{9,13},{1... | collective-permute-start | bytes 196616 | tf_op jit(solution)/shard_map/ppermute | solution.py:30
  193.0 0.8 copy-start.1

commit v5 on v4

--- a/solution.py
+++ b/solution.py
@@ -268,11 +268,11 @@
         place_now, [(rows_m1, cols_o2b)], product2, ((rows_own, tuple(cols_o0b)), (rows_m2, cols_o2b))
     )
     product2, parts1, got1 = tie((product2, parts1, got1))
-    far, v = mixed_sum(place_now, *product2, (0, 1, 2, 3, 7, 9), (4, 5, 6, 8))
-    x = far[:, 1024:]
-    d4 = send(far[:, :512], z_by(2))
-    t2, far = jnp.split(send(far[:, 512:], z_by(-2)), 2, 1)
-    d3, t3 = jnp.split(send(v, z_by(-1)), 2, 1)
+    far, v = mixed_sum(place_now, *product2, (0, 2, 3, 7, 9), (4, 5, 6, 8, 1))
+    x = far[:, 768:]
+    d4 = send(jnp.concatenate([far[:, :256], v[:, 1024:]], 1), z_by(2))
+    t2, far = jnp.split(send(far[:, 256:], z_by(-2)), 2, 1)
+    d3, t3 = jnp.split(send(v[:, :1024], z_by(-1)), 2, 1)
     x = jnp.where(first, x, far)
 
     v = over_x(*call(ys_kernel, [(SHARE, parts1[0].shape[1])] * 2, [place_now, parts1[0], *got1], 4))

time: 194 us -> 197 us (1.015)
  waiting for transfers between devices: 115 us -> 118 us
    ppermute x27, waiting for transfers between devices: 115 us -> 118 us  [send(): return lax.ppermute(value, ('aux', 'bas'), pairs)]
where the time goes in v5:
time: 197 us; the launch traced here: 196 us
  waiting for transfers between devices  118 us (60%)
  starting transfers between devices  40.2 us (20%)
  Pallas kernels  32.7 us (17%)
  local copies, waits for them, and re-layouts  4.56 us (2%)
    ppermute x27, waiting for transfers between devices, send(): return lax.ppermute(value, ('aux', 'bas'), pairs)  118 us
    ppermute x27, starting transfers between devices, send(): return lax.ppermute(value, ('aux', 'bas'), pairs)  40.2 us
    pallas_call x11, Pallas kernels, call(): pl.pallas_call(kernel, out_shape=[jax.ShapeDtypeStruct(shape, dtype) for...  32.7 us
  transfers between devices with their start and end apart: 27, of which 15 were waited for; matrix products, arithmetic and copies ran while one was open for 2% of the time, Pallas kernels for 16%

profile of v5, /device:TPU:4, one launch (start us, length us, event | category | flops | bytes accessed | tf_op | source)
XLA Modules:
  0.0 196.4 jit_solution(6264663613099049312)
XLA Ops:
  0.0 5.9 %collective-permute-start = (f32[512,1024]{1,0:T(8,128)}, f32[512,1024]{1,0:T(8,128)S(1)}, u32[]{:S(2)}, u32[]{:S(2)}) collective-permute-start(f32[512,1024]{1,0:T(8,128)} %bitcast.32), channel_id=1, source_target_pairs={{0,14},{1,15},{2,0},{3,1},{4,2},{5,3},{6,4},{7,5},{8,6},{9,7},{10,... | collective-permute-start | bytes 6291464 | tf_op jit(solution)/shard_map/ppermute | solution.py:30
  5.9 0.5 collective-permute-start.2
  6.4 1.6 copy-done
  8.0 1.4 shard_map.17
  9.5 41.6 %collective-permute-done.refs_1_ = f32[512,1024]{1,0:T(8,128)S(1)} collective-permute-done((f32[512,1024]{1,0:T(8,128)}, f32[512,1024]{1,0:T(8,128)S(1)}, u32[]{:S(2)}, u32[]{:S(2)}) %collective-permute-start) | collective-permute-done | bytes 2097184 | tf_op jit(solution)/shard_map/ppermute | solution.py:30
  51.1 3.4 %collective-permute-done.1.refs_0_ = f32[512,1024]{1,0:T(8,128)} collective-permute-done((f32[512,1024]{1,0:T(8,128)}, f32[512,1024]{1,0:T(8,128)}, u32[]{:S(2)}, u32[]{:S(2)}) %collective-permute-start.1) | collective-permute-done | bytes 2097184 | tf_op jit(solution)/shard_map/ppermute | solution.py:30
  54.9 3.0 %collective-permute-start.3 = (f32[256,1024]{1,0:T(8,128)S(1)}, f32[256,1024]{1,0:T(8,128)S(1)}, u32[]{:S(2)}, u32[]{:S(2)}) collective-permute-start(f32[256,1024]{1,0:T(8,128)S(1)} %get-tuple-element.158), channel_id=1, source_target_pairs={{0,14},{1,15},{2,0},{3,1},{4,2},{5,3},{6,4},{7,5},{8,6},{9,7},{10,... | collective-permute-start | bytes 3145736 | tf_op jit(solution)/shard_map/ppermute | solution.py:30
  57.9 1.8 fusion.4
  59.8 3.4 %shard_map.18 = (bf16[512,1024]{1,0:T(8,128)(2,1)S(1)}, bf16[512,1024]{1,0:T(8,128)(2,1)S(1)}, bf16[512,1024]{1,0:T(8,128)(2,1)S(1)}, bf16[512,1024]{1,0:T(8,128...) custom-call(s32[4]{0:T(128)S(1)} %pad_add_fusion.place_ref, ...), custom_call_target="tpu_custom_call" | custom-call | tf_op jit(solution)/shard_map/pallas_call | solution.py:54
  63.3 8.7 %shard_map.19 = (f32[256,2048]{1,0:T(8,128)S(1)}, f32[256,2048]{1,0:T(8,128)S(1)}) custom-call(s32[4]{0:T(128)S(1)} %pad_add_fusion.place_ref, bf16[512,1024]{1,0:T(8,128)(2,1)S(1)} %get-tuple-element.89.refs_0_.refs_14_.refs_4_, bf16[512,1024]{1,0:T(8,128)(2,1)S(1)} %get-tuple-element.90.refs_1_.refs_15_.refs_5_, ...), custom_call_target="tpu_custom_call" | custom-call | tf_op jit(solution)/shard_map/pallas_call | solution.py:54
  72.0 6.9 %collective-permute-done.3.refs_2_ = f32[256,1024]{1,0:T(8,128)S(1)} collective-permute-done((f32[256,1024]{1,0:T(8,128)S(1)}, f32[256,1024]{1,0:T(8,128)S(1)}, u32[]{:S(2)}, u32[]{:S(2)}) %collective-permute-start.3) | collective-permute-done | bytes 1048608 | tf_op jit(solution)/shard_map/ppermute | solution.py:30
  78.9 5.3 %collective-permute-done.4.refs_0_ = f32[256,1024]{1,0:T(8,128)S(1)} collective-permute-done((f32[256,1024]{1,0:T(8,128)S(1)}, f32[256,1024]{1,0:T(8,128)S(1)}, u32[]{:S(2)}, u32[]{:S(2)}) %collective-permute-start.4) | collective-permute-done | bytes 1048608 | tf_op jit(solution)/shard_map/ppermute | solution.py:30
  84.2 2.0 %collective-permute-start.6 = (f32[256,1024]{1,0:T(8,128)S(1)}, f32[256,1024]{1,0:T(8,128)S(1)}, u32[]{:S(2)}, u32[]{:S(2)}) collective-permute-start(f32[256,1024]{1,0:T(8,128)S(1)} %get-tuple-element.100), channel_id=1, source_target_pairs={{0,2},{1,3},{2,4},{3,5},{4,6},{5,7},{6,8},{7,9},{8,10},{9,11},{10,... | collective-permute-start | bytes 3145736 | tf_op jit(solution)/shard_map/ppermute | solution.py:30
  86.7 1.6 collective-permute-done.8.got
  88.3 0.8 shard_map.20
  89.1 20.7 %collective-permute-done.5.refs_3_ = f32[256,1024]{1,0:T(8,128)S(1)} collective-permute-done((f32[256,1024]{1,0:T(8,128)S(1)}, f32[256,1024]{1,0:T(8,128)S(1)}, u32[]{:S(2)}, u32[]{:S(2)}) %collective-permute-start.5) | collective-permute-done | bytes 1048608 | tf_op jit(solution)/shard_map/ppermute | solution.py:30
  109.7 1.2 collective-permute-done.6.refs_1_
  110.9 1.8 collective-permute-done.7.refs_4_
  113.2 1.6 collective-permute-start.10
  114.8 1.7 collective-permute-start.11
  116.4 2.0 %collective-permute-start.12 = (f32[64,2048]{1,0:T(8,128)S(1)}, f32[64,2048]{1,0:T(8,128)S(1)}, u32[]{:S(2)}, u32[]{:S(2)}) collective-permute-start(f32[64,2048]{1,0:T(8,128)S(1)} %get-tuple-element.133), channel_id=1, source_target_pairs={{0,128},{1,129},{2,130},{3,131},{4,132},{5,133},{6,134},{7,135},{8... | collective-permute-start | bytes 1572872 | tf_op jit(solution)/shard_map/ppermute | solution.py:30
  118.6 2.5 %shard_map.21 = (bf16[512,1024]{1,0:T(8,128)(2,1)S(1)}, bf16[512,1024]{1,0:T(8,128)(2,1)S(1)}, bf16[512,1024]{1,0:T(8,128)(2,1)S(1)}, bf16[512,1024]{1,0:T(8,128...) custom-call(s32[4]{0:T(128)S(1)} %pad_add_fusion.place_ref, ...), custom_call_target="tpu_custom_call" | custom-call | tf_op jit(solution)/shard_map/pallas_call | solution.py:54
  121.1 8.7 %shard_map.22 = (f32[256,2048]{1,0:T(8,128)S(1)}, f32[256,2048]{1,0:T(8,128)S(1)}) custom-call(s32[4]{0:T(128)S(1)} %pad_add_fusion.place_ref, bf16[512,1024]{1,0:T(8,128)(2,1)S(1)} %get-tuple-element.112.refs_0_, bf16[512,1024]{1,0:T(8,128)(2,1)S(1)} %get-tuple-element.113.refs_1_, bf16[512,1024]{1,0:T(8,128)(2,1)S(1)} %get-tuple-element.114.refs_2_, ...), custom_call_target="tpu_custom_call" | custom-call | tf_op jit(solution)/shard_map/pallas_call | solution.py:54
  129.8 8.6 %collective-permute-done.9.refs_0_ = f32[256,1024]{1,0:T(8,128)S(1)} collective-permute-done((f32[256,1024]{1,0:T(8,128)S(1)}, f32[256,1024]{1,0:T(8,128)S(1)}, u32[]{:S(2)}, u32[]{:S(2)}) %collective-permute-start.9) | collective-permute-done | bytes 1048608 | tf_op jit(solution)/shard_map/ppermute | solution.py:30
  138.4 0.7 shard_map.23
  139.1 2.8 %shard_map.24 = (f32[256,2560]{1,0:T(8,128)S(1)}, f32[256,2560]{1,0:T(8,128)S(1)}) custom-call(s32[4]{0:T(128)S(1)} %pad_add_fusion.place_ref, bf16[512,1024]{1,0:T(8,128)(2,1)S(1)} %get-tuple-element.87.refs_6_.refs_8_.refs_0_, bf16[512,1024]{1,0:T(8,128)(2,1)S(1)} %get-tuple-element.88.refs_7_.refs_9_.refs_1_, ...), custom_call_target="tpu_custom_call" | custom-call | tf_op jit(solution)/shard_map/pallas_call | solution.py:54
  142.0 4.9 %collective-permute-done.14.got = f32[256,2560]{1,0:T(8,128)S(1)} collective-permute-done((f32[256,2560]{1,0:T(8,128)S(1)}, f32[256,2560]{1,0:T(8,128)S(1)}, u32[]{:S(2)}, u32[]{:S(2)}) %collective-permute-start.14) | collective-permute-done | bytes 2621472 | tf_op jit(solution)/shard_map/ppermute | solution.py:30
  146.9 1.7 shard_map.26
  148.6 1.2 collective-permute-start.18
  149.8 3.2 %collective-permute-start.15 = (f32[64,1280]{1,0:T(8,128)}, f32[64,1280]{1,0:T(8,128)S(1)}, u32[]{:S(2)}, u32[]{:S(2)}) collective-permute-start(f32[64,1280]{1,0:T(8,128)} %get-tuple-element.144), channel_id=1, source_target_pairs={{0,128},{1,129},{2,130},{3,131},{4,132},{5,133},{6,134},{7,135},{8... | collective-permute-start | bytes 983048 | tf_op jit(solution)/shard_map/ppermute | solution.py:30
  153.0 0.7 collective-permute-start.16
  153.7 2.6 %collective-permute-start.17 = (f32[64,1280]{1,0:T(8,128)}, f32[64,1280]{1,0:T(8,128)S(1)}, u32[]{:S(2)}, u32[]{:S(2)}) collective-permute-start(f32[64,1280]{1,0:T(8,128)} %get-tuple-element.146), channel_id=1, source_target_pairs={{0,192},{1,193},{2,194},{3,195},{4,196},{5,197},{6,198},{7,199},{8... | collective-permute-start | bytes 983048 | tf_op jit(solution)/shard_map/ppermute | solution.py:30
  156.2 1.3 shard_map.25
  157.6 0.8 collective-permute-start.13
  158.4 12.7 %collective-permute-done.13 = f32[32,2048]{1,0:T(8,128)} collective-permute-done((f32[32,2048]{1,0:T(8,128)}, f32[32,2048]{1,0:T(8,128)}, u32[]{:S(2)}, u32[]{:S(2)}) %collective-permute-start.13) | collective-permute-done | bytes 262176 | tf_op jit(solution)/shard_map/ppermute | solution.py:30
  171.1 1.0 add.31
  172.1 1.9 collective-permute-start.21
  174.0 0.7 shard_map.27
  174.7 3.3 %collective-permute-start.22 = (f32[32,1280]{1,0:T(8,128)S(1)}, f32[32,1280]{1,0:T(8,128)S(1)}, u32[]{:S(2)}, u32[]{:S(2)}) collective-permute-start(f32[32,1280]{1,0:T(8,128)S(1)} %get-tuple-element.152), channel_id=1, source_target_pairs={{0,128},{1,129},{2,130},{3,131},{4,132},{5,133},{6,134},{7,135},{8... | collective-permute-start | bytes 491528 | tf_op jit(solution)/shard_map/ppermute | solution.py:30
  178.0 0.7 collective-permute-start.23
  178.6 2.6 %collective-permute-start.24 = (f32[32,1280]{1,0:T(8,128)S(1)}, f32[32,1280]{1,0:T(8,128)S(1)}, u32[]{:S(2)}, u32[]{:S(2)}) collective-permute-start(f32[32,1280]{1,0:T(8,128)S(1)} %get-tuple-element.154), channel_id=1, source_target_pairs={{0,192},{1,193},{2,194},{3,195},{4,196},{5,197},{6,198},{7,199},{8... | collective-permute-start | bytes 491528 | tf_op jit(solution)/shard_map/ppermute | solution.py:30
  181.2 1.2 collective-permute-start.19
  182.4 4.1 %collective-permute-done.19 = f32[32,1280]{1,0:T(8,128)S(1)} collective-permute-done((f32[32,1280]{1,0:T(8,128)S(1)}, f32[32,1280]{1,0:T(8,128)S(1)}, u32[]{:S(2)}, u32[]{:S(2)}) %collective-permute-start.19) | collective-permute-done | bytes 163872 | tf_op jit(solution)/shard_map/ppermute | solution.py:30
  186.8 3.0 %collective-permute-start.26 = (f32[32,512]{1,0:T(8,128)S(1)}, f32[32,512]{1,0:T(8,128)S(1)}, u32[]{:S(2)}, u32[]{:S(2)}) collective-permute-start(f32[32,512]{1,0:T(8,128)S(1)} %pad_maximum_fusion), channel_id=1, source_target_pairs={{0,4},{1,5},{2,6},{3,7},{4,8},{5,9},{6,10},{7,11},{8,12},{9,13},{1... | collective-permute-start | bytes 196616 | tf_op jit(solution)/shard_map/ppermute | solution.py:30
  189.8 1.2 collective-permute-start.25
  191.0 2.9 %collective-permute-done.20 = f32[32,1024]{1,0:T(8,128)S(1)} collective-permute-done((f32[32,1024]{1,0:T(8,128)S(1)}, f32[32,1024]{1,0:T(8,128)S(1)}, u32[]{:S(2)}, u32[]{:S(2)}) %collective-permute-start.20) | collective-permute-done | bytes 131104 | tf_op jit(solution)/shard_map/ppermute | solution.py:30
  194.0 1.6 collective-permute-done.25
  195.6 0.8 copy-done.1
  (43 shorter events, 2.2 us)
Async XLA Ops:
  0.0 51.1 %collective-permute-start = (f32[512,1024]{1,0:T(8,128)}, f32[512,1024]{1,0:T(8,128)S(1)}, u32[]{:S(2)}, u32[]{:S(2)}) collective-permute-start(f32[512,1024]{1,0:T(8,128)} %bitcast.32), channel_id=1, source_target_pairs={{0,14},{1,15},{2,0},{3,1},{4,2},{5,3},{6,4},{7,5},{8,6},{9,7},{10,... | collective-permute-start | bytes 6291464 | tf_op jit(solution)/shard_map/ppermute | solution.py:30
  5.9 48.6 %collective-permute-start.1 = (f32[512,1024]{1,0:T(8,128)}, f32[512,1024]{1,0:T(8,128)}, u32[]{:S(2)}, u32[]{:S(2)}) collective-permute-start(f32[512,1024]{1,0:T(8,128)} %bitcast.33), channel_id=1, source_target_pairs={{0,2},{1,3},{2,4},{3,5},{4,6},{5,7},{6,8},{7,9},{8,10},{9,11},{10,... | collective-permute-start | bytes 6291464 | tf_op jit(solution)/shard_map/ppermute | solution.py:30
  5.9 48.9 %collective-permute-start.2 = (f32[512,1024]{1,0:T(8,128)}, f32[512,1024]{1,0:T(8,128)}, u32[]{:S(2)}, u32[]{:S(2)}) collective-permute-start(f32[512,1024]{1,0:T(8,128)} %bitcast.34), channel_id=1, source_target_pairs={{0,1},{1,0},{2,3},{3,2},{4,5},{5,4},{6,7},{7,6},{8,9},{9,8},{10,11... | collective-permute-start | bytes 6291464 | tf_op jit(solution)/shard_map/ppermute | solution.py:30
  6.4 1.6 copy-start
  54.9 24.0 %collective-permute-start.3 = (f32[256,1024]{1,0:T(8,128)S(1)}, f32[256,1024]{1,0:T(8,128)S(1)}, u32[]{:S(2)}, u32[]{:S(2)}) collective-permute-start(f32[256,1024]{1,0:T(8,128)S(1)} %get-tuple-element.158), channel_id=1, source_target_pairs={{0,14},{1,15},{2,0},{3,1},{4,2},{5,3},{6,4},{7,5},{8,6},{9,7},{10,... | collective-permute-start | bytes 3145736 | tf_op jit(solution)/shard_map/ppermute | solution.py:30
  59.7 24.4 %collective-permute-start.4 = (f32[256,1024]{1,0:T(8,128)S(1)}, f32[256,1024]{1,0:T(8,128)S(1)}, u32[]{:S(2)}, u32[]{:S(2)}) collective-permute-start(f32[256,1024]{1,0:T(8,128)S(1)} %get-tuple-element.156), channel_id=1, source_target_pairs={{0,2},{1,3},{2,4},{3,5},{4,6},{5,7},{6,8},{7,9},{8,10},{9,11},{10,... | collective-permute-start | bytes 3145736 | tf_op jit(solution)/shard_map/ppermute | solution.py:30
  84.1 4.2 %collective-permute-start.8 = (f32[256,2048]{1,0:T(8,128)S(1)}, f32[256,2048]{1,0:T(8,128)S(1)}, u32[]{:S(2)}, u32[]{:S(2)}) collective-permute-start(f32[256,2048]{1,0:T(8,128)S(1)} %get-tuple-element.103), channel_id=1, source_target_pairs={{0,16},{1,17},{2,18},{3,19},{4,20},{5,21},{6,22},{7,23},{8,24},{9,... | collective-permute-start | bytes 6291464 | tf_op jit(solution)/shard_map/ppermute | solution.py:30
  84.2 25.6 %collective-permute-start.5 = (f32[256,1024]{1,0:T(8,128)S(1)}, f32[256,1024]{1,0:T(8,128)S(1)}, u32[]{:S(2)}, u32[]{:S(2)}) collective-permute-start(f32[256,1024]{1,0:T(8,128)S(1)} %get-tuple-element.99), channel_id=1, source_target_pairs={{0,14},{1,15},{2,0},{3,1},{4,2},{5,3},{6,4},{7,5},{8,6},{9,7},{10,... | collective-permute-start | bytes 3145736 | tf_op jit(solution)/shard_map/ppermute | solution.py:30
  84.2 26.8 %collective-permute-start.6 = (f32[256,1024]{1,0:T(8,128)S(1)}, f32[256,1024]{1,0:T(8,128)S(1)}, u32[]{:S(2)}, u32[]{:S(2)}) collective-permute-start(f32[256,1024]{1,0:T(8,128)S(1)} %get-tuple-element.100), channel_id=1, source_target_pairs={{0,2},{1,3},{2,4},{3,5},{4,6},{5,7},{6,8},{7,9},{8,10},{9,11},{10,... | collective-permute-start | bytes 3145736 | tf_op jit(solution)/shard_map/ppermute | solution.py:30
  86.2 26.5 %collective-permute-start.7 = (f32[256,1024]{1,0:T(8,128)S(1)}, f32[256,1024]{1,0:T(8,128)S(1)}, u32[]{:S(2)}, u32[]{:S(2)}) collective-permute-start(f32[256,1024]{1,0:T(8,128)S(1)} %collective-permute-done.3.refs_2_), channel_id=1, source_target_pairs={{0,1},{1,0},{2,3},{3,2},{4,5},{5,4},{6,7},{7,6},{8,9},{9,8},{10,11... | collective-permute-start | bytes 3145736 | tf_op jit(solution)/shard_map/ppermute | solution.py:30
  112.7 25.7 %collective-permute-start.9 = (f32[256,1024]{1,0:T(8,128)S(1)}, f32[256,1024]{1,0:T(8,128)S(1)}, u32[]{:S(2)}, u32[]{:S(2)}) collective-permute-start(f32[256,1024]{1,0:T(8,128)S(1)} %collective-permute-done.5.refs_3_), channel_id=1, source_target_pairs={{0,1},{1,0},{2,3},{3,2},{4,5},{5,4},{6,7},{7,6},{8,9},{9,8},{10,11... | collective-permute-start | bytes 3145736 | tf_op jit(solution)/shard_map/ppermute | solution.py:30
  113.2 28.7 %collective-permute-start.10 = (f32[64,2048]{1,0:T(8,128)S(1)}, f32[64,2048]{1,0:T(8,128)S(1)}, u32[]{:S(2)}, u32[]{:S(2)}) collective-permute-start(f32[64,2048]{1,0:T(8,128)S(1)} %get-tuple-element.132), channel_id=1, source_target_pairs={{0,64},{1,65},{2,66},{3,67},{4,68},{5,69},{6,70},{7,71},{8,72},{9,... | collective-permute-start | bytes 1572872 | tf_op jit(solution)/shard_map/ppermute | solution.py:30
  114.8 27.1 %collective-permute-start.11 = (f32[64,2048]{1,0:T(8,128)S(1)}, f32[64,2048]{1,0:T(8,128)S(1)}, u32[]{:S(2)}, u32[]{:S(2)}) collective-permute-start(f32[64,2048]{1,0:T(8,128)S(1)} %get-tuple-element.134), channel_id=1, source_target_pairs={{0,192},{1,193},{2,194},{3,195},{4,196},{5,197},{6,198},{7,199},{8... | collective-permute-start | bytes 1572872 | tf_op jit(solution)/shard_map/ppermute | solution.py:30
  116.4 25.5 %collective-permute-start.12 = (f32[64,2048]{1,0:T(8,128)S(1)}, f32[64,2048]{1,0:T(8,128)S(1)}, u32[]{:S(2)}, u32[]{:S(2)}) collective-permute-start(f32[64,2048]{1,0:T(8,128)S(1)} %get-tuple-element.133), channel_id=1, source_target_pairs={{0,128},{1,129},{2,130},{3,131},{4,132},{5,133},{6,134},{7,135},{8... | collective-permute-start | bytes 1572872 | tf_op jit(solution)/shard_map/ppermute | solution.py:30
  141.9 5.0 %collective-permute-start.14 = (f32[256,2560]{1,0:T(8,128)S(1)}, f32[256,2560]{1,0:T(8,128)S(1)}, u32[]{:S(2)}, u32[]{:S(2)}) collective-permute-start(f32[256,2560]{1,0:T(8,128)S(1)} %get-tuple-element.142), channel_id=1, source_target_pairs={{0,16},{1,17},{2,18},{3,19},{4,20},{5,21},{6,22},{7,23},{8,24},{9,... | collective-permute-start | bytes 7864328 | tf_op jit(solution)/shard_map/ppermute | solution.py:30
  148.6 25.4 %collective-permute-start.18 = (f32[128,1280]{1,0:T(8,128)S(1)}, f32[128,1280]{1,0:T(8,128)S(1)}, u32[]{:S(2)}, u32[]{:S(2)}) collective-permute-start(f32[128,1280]{1,0:T(8,128)S(1)} %get-tuple-element.148), channel_id=1, source_target_pairs={{0,32},{1,33},{2,34},{3,35},{4,36},{5,37},{6,38},{7,39},{8,40},{9,... | collective-permute-start | bytes 1966088 | tf_op jit(solution)/shard_map/ppermute | solution.py:30
  149.8 24.2 %collective-permute-start.15 = (f32[64,1280]{1,0:T(8,128)}, f32[64,1280]{1,0:T(8,128)S(1)}, u32[]{:S(2)}, u32[]{:S(2)}) collective-permute-start(f32[64,1280]{1,0:T(8,128)} %get-tuple-element.144), channel_id=1, source_target_pairs={{0,128},{1,129},{2,130},{3,131},{4,132},{5,133},{6,134},{7,135},{8... | collective-permute-start | bytes 983048 | tf_op jit(solution)/shard_map/ppermute | solution.py:30
  153.0 21.0 %collective-permute-start.16 = (f32[64,1280]{1,0:T(8,128)}, f32[64,1280]{1,0:T(8,128)S(1)}, u32[]{:S(2)}, u32[]{:S(2)}) collective-permute-start(f32[64,1280]{1,0:T(8,128)} %get-tuple-element.145), channel_id=1, source_target_pairs={{0,64},{1,65},{2,66},{3,67},{4,68},{5,69},{6,70},{7,71},{8,72},{9,... | collective-permute-start | bytes 983048 | tf_op jit(solution)/shard_map/ppermute | solution.py:30
  153.7 20.3 %collective-permute-start.17 = (f32[64,1280]{1,0:T(8,128)}, f32[64,1280]{1,0:T(8,128)S(1)}, u32[]{:S(2)}, u32[]{:S(2)}) collective-permute-start(f32[64,1280]{1,0:T(8,128)} %get-tuple-element.146), channel_id=1, source_target_pairs={{0,192},{1,193},{2,194},{3,195},{4,196},{5,197},{6,198},{7,199},{8... | collective-permute-start | bytes 983048 | tf_op jit(solution)/shard_map/ppermute | solution.py:30
  157.6 13.5 %collective-permute-start.13 = (f32[32,2048]{1,0:T(8,128)}, f32[32,2048]{1,0:T(8,128)}, u32[]{:S(2)}, u32[]{:S(2)}) collective-permute-start(f32[32,2048]{1,0:T(8,128)} %get-tuple-element.140), channel_id=1, source_target_pairs={{0,32},{1,33},{2,34},{3,35},{4,36},{5,37},{6,38},{7,39},{8,40},{9,... | collective-permute-start | bytes 786440 | tf_op jit(solution)/shard_map/ppermute | solution.py:30
  172.1 18.9 %collective-permute-start.21 = (f32[32,1024]{1,0:T(8,128)S(1)}, f32[32,1024]{1,0:T(8,128)S(1)}, u32[]{:S(2)}, u32[]{:S(2)}) collective-permute-start(f32[32,1024]{1,0:T(8,128)S(1)} %slice.61), channel_id=1, source_target_pairs={{0,14},{1,15},{2,0},{3,1},{4,2},{5,3},{6,4},{7,5},{8,6},{9,7},{10,... | collective-permute-start | bytes 393224 | tf_op jit(solution)/shard_map/ppermute | solution.py:30
  174.7 12.0 %collective-permute-start.22 = (f32[32,1280]{1,0:T(8,128)S(1)}, f32[32,1280]{1,0:T(8,128)S(1)}, u32[]{:S(2)}, u32[]{:S(2)}) collective-permute-start(f32[32,1280]{1,0:T(8,128)S(1)} %get-tuple-element.152), channel_id=1, source_target_pairs={{0,128},{1,129},{2,130},{3,131},{4,132},{5,133},{6,134},{7,135},{8... | collective-permute-start | bytes 491528 | tf_op jit(solution)/shard_map/ppermute | solution.py:30
  178.0 8.7 %collective-permute-start.23 = (f32[32,1280]{1,0:T(8,128)S(1)}, f32[32,1280]{1,0:T(8,128)S(1)}, u32[]{:S(2)}, u32[]{:S(2)}) collective-permute-start(f32[32,1280]{1,0:T(8,128)S(1)} %get-tuple-element.153), channel_id=1, source_target_pairs={{0,64},{1,65},{2,66},{3,67},{4,68},{5,69},{6,70},{7,71},{8,72},{9,... | collective-permute-start | bytes 491528 | tf_op jit(solution)/shard_map/ppermute | solution.py:30
  178.6 8.0 %collective-permute-start.24 = (f32[32,1280]{1,0:T(8,128)S(1)}, f32[32,1280]{1,0:T(8,128)S(1)}, u32[]{:S(2)}, u32[]{:S(2)}) collective-permute-start(f32[32,1280]{1,0:T(8,128)S(1)} %get-tuple-element.154), channel_id=1, source_target_pairs={{0,192},{1,193},{2,194},{3,195},{4,196},{5,197},{6,198},{7,199},{8... | collective-permute-start | bytes 491528 | tf_op jit(solution)/shard_map/ppermute | solution.py:30
  181.2 5.3 %collective-permute-start.19 = (f32[32,1280]{1,0:T(8,128)S(1)}, f32[32,1280]{1,0:T(8,128)S(1)}, u32[]{:S(2)}, u32[]{:S(2)}) collective-permute-start(f32[32,1280]{1,0:T(8,128)S(1)} %get-tuple-element.150), channel_id=1, source_target_pairs={{0,32},{1,33},{2,34},{3,35},{4,36},{5,37},{6,38},{7,39},{8,40},{9,... | collective-permute-start | bytes 491528 | tf_op jit(solution)/shard_map/ppermute | solution.py:30
  186.6 7.3 %collective-permute-start.20 = (f32[32,1024]{1,0:T(8,128)S(1)}, f32[32,1024]{1,0:T(8,128)S(1)}, u32[]{:S(2)}, u32[]{:S(2)}) collective-permute-start(f32[32,1024]{1,0:T(8,128)S(1)} %slice.60), channel_id=1, source_target_pairs={{0,12},{1,13},{2,14},{3,15},{4,0},{5,1},{6,2},{7,3},{8,4},{9,5},{1... | collective-permute-start | bytes 393224 | tf_op jit(solution)/shard_map/ppermute | solution.py:30
  186.8 8.8 %collective-permute-start.26 = (f32[32,512]{1,0:T(8,128)S(1)}, f32[32,512]{1,0:T(8,128)S(1)}, u32[]{:S(2)}, u32[]{:S(2)}) collective-permute-start(f32[32,512]{1,0:T(8,128)S(1)} %pad_maximum_fusion), channel_id=1, source_target_pairs={{0,4},{1,5},{2,6},{3,7},{4,8},{5,9},{6,10},{7,11},{8,12},{9,13},{1... | collective-permute-start | bytes 196616 | tf_op jit(solution)/shard_map/ppermute | solution.py:30
  189.8 5.8 %collective-permute-start.25 = (f32[32,1024]{1,0:T(8,128)S(1)}, f32[32,1024]{1,0:T(8,128)S(1)}, u32[]{:S(2)}, u32[]{:S(2)}) collective-permute-start(f32[32,1024]{1,0:T(8,128)S(1)} %slice.62), channel_id=1, source_target_pairs={{0,14},{1,15},{2,0},{3,1},{4,2},{5,3},{6,4},{7,5},{8,6},{9,7},{10,... | collective-permute-start | bytes 393224 | tf_op jit(solution)/shard_map/ppermute | solution.py:30
  195.6 0.8 copy-start.1
